TPU v7x, 32 devices: a whole 2x2x4 slice. The times are simulated.
32 devices in a mesh: clu: 8 (over z, y), rk: 4 (over x, core).
Axes of the slice: x: 2, y: 2, z: 4, core: 2. Of those that a mesh axis runs over, the one named last changes fastest.
Arguments:
- bases: float32 [8, 32, 256, 64], P('clu', None, None, 'rk'), may hold values from -0.4 to 0.4
- leaf_transfer: float32 [8, 32, 64, 64], P('clu')
- node_transfer: float32 [8, 64, 64], P('clu'), as said below
- pair_transfer: float32 [8, 64, 64], P('clu'), as said below
- quad_transfer: float32 [8, 64, 64], P('clu'), as said below
- coupling: float32 [8, 32, 32, 64, 64], P('clu', None, None, 'rk'), may hold values from -1.2 to 1.2
- row_device: int32 [8, 32, 32, 1], P('clu'), may hold values from 0 to 7; in each aligned block of 1024 rows (0 to 1023, 1024 to 2047, ..., all dimensions but the last counted through in order) at most 192 rows name the same one
- row_slot: int32 [8, 32, 32], P('clu'), may hold values from 0 to 31
- block_count: int32 [8, 32], P('clu'), may hold values from 16 to 32
Outputs:
- leaf_weights: float32 [8, 32, 64, 64], P('clu', None, None, 'rk')
- node_weights: float32 [4, 8, 64, 64], P(None, 'clu', None, 'rk')
- coupled: float32 [8, 32, 64, 64], P('clu', None, None, 'rk')
Inputs may be any that keep to these rules, and one draw needn't show every extreme that they name: node_transfer[c] is drawn anew for every clu index. pair_transfer[c] equals pair_transfer[c xor 1]: one matrix for each node over two clu indices. quad_transfer[c] is the same for the four clu indices c of one node (equal c // 4). Among the 1024 listed blocks of one clu index, at most 192 name the same row_device.
All inputs are finite; a program needn't handle non-finite values.
Results may differ from a plain program's by a relative error of at most 0.00014.
Values sent between devices are 32-bit elements; how exact they have to be, the bound alone decides.
A program may use at most 128 MiB of HBM per device.

v0:
```python
import jax
import jax.numpy as jnp
from jax import lax
from jax.sharding import PartitionSpec as P


def from_partner(value, axis, bit):
    mask = 2**bit
    pairs = [(source, source ^ mask) for source in range(lax.axis_size(axis))]
    return lax.ppermute(value, axis, pairs)


def upper_factor(gram):
    return jnp.swapaxes(jnp.linalg.cholesky(gram), -1, -2)


def shards(
    bases,
    leaf_transfer,
    node_transfer,
    pair_transfer,
    quad_transfer,
    coupling,
    row_device,
    row_slot,
    block_count,
):
    highest = lax.Precision.HIGHEST
    n_rank = lax.axis_size("rk")
    rank_index = lax.axis_index("rk")
    local = bases[0]
    leaves = local.shape[0]
    width = local.shape[2]
    full_rank = width * n_rank
    whole = lax.all_gather(local, "rk", axis=2, tiled=True)
    gram = jnp.einsum("jpa,jpb->jab", whole, whole, precision=highest)
    leaf_moves = leaf_transfer[0]
    moved = jnp.einsum("jab,jbe->jae", gram, leaf_moves, precision=highest)
    term = jnp.einsum("jaf,jae->jfe", leaf_moves, moved, precision=highest)
    level = jnp.sum(term, axis=0)
    grams = [level]
    for bit, transfer in enumerate((node_transfer[0], pair_transfer[0], quad_transfer[0])):
        moved = jnp.dot(level, transfer, precision=highest)
        term = jnp.dot(transfer.T, moved, precision=highest)
        level = term + from_partner(term, "clu", bit)
        grams.append(level)
    factor_all = upper_factor(jnp.concatenate([gram, jnp.stack(grams)], axis=0))
    leaf_factor = factor_all[:leaves]
    node_factors = factor_all[leaves:]
    node_weights = lax.dynamic_slice_in_dim(node_factors, rank_index * width, width, 2)
    leaf_weights = lax.dynamic_slice_in_dim(leaf_factor, rank_index * width, width, 2)
    blocks = coupling[0]
    listed = blocks.shape[1]
    prod = jnp.einsum("jkab,jcb->jkac", blocks, leaf_factor, precision=highest)
    count = leaves * listed
    feature = width * full_rank
    flat = prod.reshape(count, feature)
    dest = row_device[0, :, :, 0].reshape(count)
    slot = row_slot[0].reshape(count)
    valid = (jnp.arange(listed, dtype=jnp.int32)[None, :] < block_count[0][:, None]).reshape(count)
    n_clu = lax.axis_size("clu")
    capacity = 3 * count // (2 * n_clu)
    owners_table = jnp.arange(n_clu, dtype=jnp.int32)[None, :]
    onehot = ((dest[:, None] == owners_table) & valid[:, None]).astype(jnp.int32)
    before = jnp.cumsum(onehot, axis=0) - onehot
    place = jnp.sum(before * onehot, axis=1)
    target = jnp.where(valid, dest * capacity + place, n_clu * capacity)
    buffer = jnp.zeros((n_clu * capacity + 1, feature), jnp.float32).at[target].set(flat)
    buffer = buffer[:-1].reshape(n_clu, capacity, feature)
    labels = jnp.full((n_clu * capacity + 1,), float(leaves), jnp.float32)
    labels = labels.at[target].set(jnp.where(valid, slot, leaves).astype(jnp.float32))
    labels = labels[:-1].reshape(n_clu, capacity)
    arrived, owners = (
        lax.all_to_all(buffer, "clu", split_axis=0, concat_axis=0, tiled=True),
        lax.all_to_all(labels, "clu", split_axis=0, concat_axis=0, tiled=True),
    )
    owner_ids = owners.reshape(-1).astype(jnp.int32)
    summed = jax.ops.segment_sum(arrived.reshape(-1, feature), owner_ids, num_segments=leaves + 1)[
        :leaves
    ]
    gathered = summed.reshape(leaves, width, full_rank)
    partial_sum = jnp.einsum("jab,jbe->jae", leaf_weights, gathered, precision=highest)
    coupled = lax.psum_scatter(partial_sum, "rk", scatter_dimension=2, tiled=True)
    return (leaf_weights[None], node_weights[:, None], coupled[None])


def solution(mesh):
    placed = (
        P("clu", None, None, "rk"),
        P("clu", None, None, None),
        P("clu", None, None),
        P("clu", None, None),
        P("clu", None, None),
        P("clu", None, None, "rk", None),
        P("clu", None, None, None),
        P("clu", None, None),
        P("clu", None),
    )
    return jax.shard_map(
        shards,
        mesh=mesh,
        in_specs=placed,
        out_specs=(
            P("clu", None, None, "rk"),
            P(None, "clu", None, "rk"),
            P("clu", None, None, "rk"),
        ),
        check_vma=False,
    )
```

profile of v0, /device:TPU:0, one launch (start us, length us, event | category | flops | bytes accessed | tf_op | source)
XLA Modules:
  0.0 510.5 jit_solution(299467973722780290)
XLA Ops:
  11.8 2.3 reduce-window.6
  14.5 1.4 fusion.41
  17.0 4.3 scatter_custom_fusion
  22.0 7.3 %all-to-all-start = ((f32[8,1,192]{2,1,0:T(1,128)}), f32[8,1,192]{2,1,0:T(1,128)S(1)}, u32[]{:S(2)}, u32[]{:S(2)}) async-start(f32[8,1,192]{2,1,0:T(1,128)} %all_to_all.9), calls=%async_computation | async-start | bytes 16384 | tf_op jit(solution)/shard_map/all_to_all | solution.py:75
  29.3 5.5 %all-gather.3.cloned.1.call-done = f32[1,32,256,64]{2,3,1,0:T(8,128)} async-done(((f32[1,32,256,16]{2,3,1,0:T(8,128)}), f32[1,32,256,64]{2,3,1,0:T(8,128)}) %all-gather.3.cloned.1.call-update) | async-done | bytes 2097168 | tf_op jit(solution)/shard_map/all_gather | solution.py:35
  34.9 4.2 fusion.7
  41.8 1.9 fusion.13
  45.3 1.5 collective-permute-start
  46.8 2.4 collective-permute-done
  49.8 1.6 collective-permute-start.1
  51.3 2.4 collective-permute-done.1
  54.2 2.5 collective-permute-start.2
  56.7 2.4 collective-permute-done.2
  60.7 211.7 %custom-call.4 = f32[36,64,64]{2,1,0:T(8,128)S(1)} custom-call(f32[36,64,64]{2,1,0:T(8,128)} %fusion.9), custom_call_target="Cholesky" | custom-call | tf_op jit(solution)/shard_map/jit(cholesky)/cholesky | solution.py:14
  272.8 13.7 %fusion.2 = f32[32,32,16,64]{3,1,2,0:T(8,128)S(1)} fusion(f32[32,32,16,64]{3,2,1,0:T(8,128)} %bitcast.100, f32[36,64,64]{1,2,0:T(8,128)S(1)} %select_bitcast_fusion), kind=kOutput, calls=%fused_computation.5 | convolution fusion | flops 805306368 | bytes 9437184 | tf_op jit(solution)/shard_map/jkab,jcb->jkac/dot_general | solution.py:54
  286.5 10.8 %copy.26 = f32[32,32,16,64]{3,2,1,0:T(8,128)} copy(f32[32,32,16,64]{3,1,2,0:T(8,128)S(1)} %fusion.2) | data formatting | bytes 8388608 | tf_op jit(solution)/shard_map/jkab,jcb->jkac/dot_general | solution.py:54
  297.3 7.6 %reshape.148 = f32[1024,1024]{1,0:T(8,128)} reshape(f32[32,32,16,64]{3,2,1,0:T(8,128)} %copy.26) | data formatting | bytes 8388608 | tf_op jit(solution)/shard_map/reshape | solution.py:57
  304.9 8.8 %scatter_custom_fusion.1 = f32[1537,1024]{1,0:T(8,128)} fusion(s32[1024]{0:T(1024)S(1)} %bitcast.106, f32[1024,1024]{1,0:T(8,128)} %reshape.148, f32[]{:T(128)} %constant.55.clone.1), kind=kCustom, calls=%fused_computation.6 | custom fusion | bytes 6296064 | tf_op jit(solution)/shard_map/scatter | solution.py:68
  313.7 6.6 %slice.38 = f32[1536,1024]{1,0:T(8,128)} slice(f32[1537,1024]{1,0:T(8,128)} %scatter_custom_fusion.1), slice={[0:1536], [0:1024]} | slice | bytes 12582912 | tf_op jit(solution)/shard_map/slice | solution.py:69
  320.3 5.8 %all-to-all-start.1 = ((f32[8,192,1024]{2,1,0:T(8,128)}), f32[8,192,1024]{2,1,0:T(8,128)}, u32[]{:S(2)}, u32[]{:S(2)}) async-start(f32[8,192,1024]{2,1,0:T(8,128)} %bitcast.99), calls=%async_computation.1 | async-start | bytes 12582912 | tf_op jit(solution)/shard_map/all_to_all | solution.py:74
  326.4 134.9 %all-to-all-done.1 = f32[8,192,1024]{2,1,0:T(8,128)} async-done(((f32[8,192,1024]{2,1,0:T(8,128)}), f32[8,192,1024]{2,1,0:T(8,128)}, u32[]{:S(2)}, u32[]{:S(2)}) %all-to-all-start.1) | async-done | bytes 6291488 | tf_op jit(solution)/shard_map/all_to_all | solution.py:74
  461.3 14.7 %scatter_custom_fusion.2 = f32[33,1024]{1,0:T(8,128)S(1)} fusion(s32[1536]{0:T(1024)S(1)} %reshape.154, f32[1536,1024]{1,0:T(8,128)} %bitcast.26, f32[]{:T(128)} %constant.55.clone.1), kind=kCustom, calls=%fused_computation.25 | custom fusion | flops 1572864 | bytes 135680 | tf_op jit(solution)/shard_map/scatter-add | solution.py:78
  477.7 2.8 fusion.15
  481.9 21.8 %reduce-scatter.2.cloned.1.call-done = f32[32,64,16]{1,2,0:T(8,128)} async-done(((f32[32,64,64]{1,2,0:T(8,128)}), f32[32,64,16]{1,2,0:T(8,128)}) %reduce-scatter.2.cloned.1.call-update) | async-done | bytes 131088 | tf_op jit(solution)/shard_map/reduce_scatter | solution.py:83
  (63 shorter events, 17.3 us)
Async XLA Ops:
  7.2 34.6 %copy-start = (f32[1,32,64,64]{3,2,1,0:T(8,128)S(1)}, f32[1,32,64,64]{3,2,1,0:T(8,128)}, u32[]{:S(2)}) copy-start(f32[1,32,64,64]{3,2,1,0:T(8,128)} %param.10) | copy-start | bytes 1572868
  7.2 27.7 %all-gather.3.cloned.1.call-start = ((), (), s32[]{:S(2)}) async-start(), calls=%async_computation.4 | async-start | bytes 2621440 | tf_op jit(solution)/shard_map/all_gather | solution.py:35
  22.0 298.3 %all-to-all-start = ((f32[8,1,192]{2,1,0:T(1,128)}), f32[8,1,192]{2,1,0:T(1,128)S(1)}, u32[]{:S(2)}, u32[]{:S(2)}) async-start(f32[8,1,192]{2,1,0:T(1,128)} %all_to_all.9), calls=%async_computation | async-start | bytes 16384 | tf_op jit(solution)/shard_map/all_to_all | solution.py:75
  43.7 1.1 copy-start.1
  43.7 5.6 %copy-start.2 = (f32[1,64,64]{2,1,0:T(8,128)S(1)}, f32[1,64,64]{2,1,0:T(8,128)}, u32[]{:S(2)}) copy-start(f32[1,64,64]{2,1,0:T(8,128)} %param.12) | copy-start | bytes 49156
  43.7 10.1 %copy-start.3 = (f32[1,64,64]{2,1,0:T(8,128)S(1)}, f32[1,64,64]{2,1,0:T(8,128)}, u32[]{:S(2)}) copy-start(f32[1,64,64]{2,1,0:T(8,128)} %param.13) | copy-start | bytes 49156
  45.3 4.0 collective-permute-start
  49.8 4.0 collective-permute-start.1
  54.2 4.9 collective-permute-start.2
  320.3 141.0 %all-to-all-start.1 = ((f32[8,192,1024]{2,1,0:T(8,128)}), f32[8,192,1024]{2,1,0:T(8,128)}, u32[]{:S(2)}, u32[]{:S(2)}) async-start(f32[8,192,1024]{2,1,0:T(8,128)} %bitcast.99), calls=%async_computation.1 | async-start | bytes 12582912 | tf_op jit(solution)/shard_map/all_to_all | solution.py:74
  326.2 177.5 %reduce-scatter.2.cloned.1.call-start = ((), (), s32[]{:S(2)}) async-start(), calls=%async_computation.3 | async-start | bytes 1310720 | tf_op jit(solution)/shard_map/reduce_scatter | solution.py:83
Sparse Core Ops, SparseCore 0:
  9.6 25.2 all-gather.2
  480.7 23.0 reduce-scatter.1
where the time goes:
time: 511 us
  other arithmetic  234 us (46%)
  waiting for transfers between devices  170 us (33%)
  local copies, waits for them, and re-layouts  48.1 us (9%)
  matrix products  25.1 us (5%)
  starting transfers between devices  18.8 us (4%)
  between operations  14.3 us (3%)
    another operation x4, other arithmetic, upper_factor(): return jnp.swapaxes(jnp.linalg.cholesky(gram), -1, -2)  212 us
    all_to_all x1, waiting for transfers between devices, shards(): lax.all_to_all(buffer, 'clu', split_axis=0, concat_axis=0, tiled=True)  135 us
    reduce_scatter x1, waiting for transfers between devices, shards(): lax.psum_scatter(partial_sum, 'rk', scatter_dimension=2, tiled=True)  21.8 us
    scatter-add x1, other arithmetic, shards(): jax.ops.segment_sum(arrived.reshape(-1, feature), owner_ids, num_segments...  14.7 us
    dot_general x1, matrix products, shards(): prod = jnp.einsum('jkab,jcb->jkac', blocks, leaf_factor, precision=highest)  13.7 us
    dot_general x1, local copies, waits for them, and re-layouts, shards(): prod = jnp.einsum('jkab,jcb->jkac', blocks, leaf_factor, precision=highest)  10.8 us
  transfers between devices with their start and end apart: 7, of which 6 were waited for; matrix products, arithmetic and copies ran while one was open for 56% of the time, Pallas kernels for 0%

commit v1 on v0

v1 whole, which is shorter than its diff:
```python
import functools

import jax
import jax.numpy as jnp
from jax import lax
from jax.experimental import pallas as pl
from jax.experimental.pallas import tpu as pltpu
from jax.sharding import PartitionSpec as P

HIGHEST = lax.Precision.HIGHEST
F32 = jnp.float32
BF16 = jnp.bfloat16
CHUNKS = 4
BATCH = 8


def dot(a, b, precision=None):
    return jnp.dot(a, b, precision=precision, preferred_element_type=F32)


def dot_nt(a, b):
    return lax.dot_general(a, b, (((1,), (1,)), ((), ())), precision=HIGHEST, preferred_element_type=F32)


def dot_tn(a, b):
    return lax.dot_general(a, b, (((0,), (0,)), ((), ())), precision=HIGHEST, preferred_element_type=F32)


def split(x):
    high = x.astype(BF16)
    return high, (x - high.astype(F32)).astype(BF16)


def factor_batch(rank, gram_ref, cols, upper_ref):
    @pl.loop(0, rank, unroll=8)
    def _(i):
        cols[i] = gram_ref[pl.ds(pl.multiple_of(i * BATCH, BATCH), BATCH), :].T

    step = 4
    for k0 in range(0, rank, step):
        r0 = k0 // 8 * 8

        def body(group, accs):
            accs = list(accs)
            for s in range(step):
                j = group * step + s
                col = cols[j, r0:, :]
                for t in range(step):
                    accs[t] = accs[t] - col * cols[j, k0 + t : k0 + t + 1, :]
            return tuple(accs)

        accs = tuple(cols[k0 + t, r0:, :] for t in range(step))
        accs = list(lax.fori_loop(0, k0 // step, body, accs))
        for t in range(step):
            at = k0 + t - r0
            col = accs[t] * lax.rsqrt(accs[t][at : at + 1, :])
            cols[k0 + t, r0:, :] = col
            for u in range(t + 1, step):
                to = k0 + u - r0
                accs[u] = accs[u] - col * col[to : to + 1, :]

    lane = lax.broadcasted_iota(jnp.int32, (BATCH, rank), 1)

    @pl.loop(0, rank, unroll=8)
    def _(k):
        row = cols[k].T
        upper_ref[pl.ds(pl.multiple_of(k * BATCH, BATCH), BATCH), :] = jnp.where(lane >= k, row, 0.0)


def kernel(
    n_clu,
    n_rk,
    leaves,
    listed,
    width,
    bases_ref,
    coup_ref,
    leaf_move_ref,
    node_ref,
    pair_ref,
    quad_ref,
    target_ref,
    lw_ref,
    nw_ref,
    cp_ref,
    bas,
    coup,
    moves,
    x_buf,
    onehot,
    gram_rows,
    cols,
    upper,
    grams,
    low_packed,
    low_own,
    p_high,
    p_low,
    acc,
    arrived,
    mine,
    theirs,
    out_send,
    out_recv,
    g1,
    term_send,
    term_recv,
    low_node,
    local_sem,
    bas_s,
    bas_r,
    low_s,
    low_r,
    g1_s,
    g1_r,
    lev_s,
    lev_r,
    rs_s,
    rs_r,
    mine_s,
    mine_r,
    out_s,
    out_r,
):
    rank = width * n_rk
    half = rank // 2
    group = leaves // n_rk
    pairs = width // 2
    count = leaves * listed
    feature = width * rank
    part = feature // CHUNKS
    q = lax.axis_index("rk")
    me = lax.axis_index("clu")

    def rk_peer(d):
        return lax.rem(q + d, n_rk)

    def clu_peer(d):
        return lax.rem(me + d, n_clu)

    def to_rk(src, dst, send, recv, d):
        return pltpu.make_async_remote_copy(
            src_ref=src,
            dst_ref=dst,
            send_sem=send.at[d],
            recv_sem=recv.at[d],
            device_id={"rk": rk_peer(d)},
            device_id_type=pl.DeviceIdType.MESH,
        )

    blocks = leaves // CHUNKS
    loads = []
    for c in range(CHUNKS):
        rows = pl.ds(c * blocks, blocks)
        loads.append(pltpu.make_async_copy(coup_ref.at[rows], coup.at[rows], local_sem.at[c]))
        loads[-1].start()
    own_rows = pl.ds(q * group, group)
    own_bases = pltpu.make_async_copy(bases_ref.at[own_rows], bas.at[q], local_sem.at[CHUNKS])
    own_bases.start()
    own_moves = pltpu.make_async_copy(leaf_move_ref.at[own_rows], moves, local_sem.at[CHUNKS + 1])
    own_moves.start()

    barrier = pltpu.get_barrier_semaphore()
    for d in range(1, n_rk):
        pl.semaphore_signal(barrier, inc=1, device_id={"rk": rk_peer(d)}, device_id_type=pl.DeviceIdType.MESH)
    for d in range(1, n_clu):
        pl.semaphore_signal(barrier, inc=1, device_id={"clu": clu_peer(d)}, device_id_type=pl.DeviceIdType.MESH)
    pl.semaphore_wait(barrier, n_rk + n_clu - 2)

    base_copies = [
        to_rk(bases_ref.at[pl.ds(rk_peer(d) * group, group)], bas.at[q], bas_s, bas_r, d) for d in range(1, n_rk)
    ]
    for copy in base_copies:
        copy.start()

    block_rows = 8 * leaves
    for first in range(0, n_clu * leaves, block_rows):
        size = min(block_rows, n_clu * leaves - first)
        owner = lax.broadcasted_iota(jnp.int32, (size, count), 0) + first
        onehot[first : first + size, :] = jnp.where(owner == target_ref[...], 1.0, 0.0).astype(BF16)

    for c in range(CHUNKS):
        loads[c].wait()

        @pl.loop(c * blocks, (c + 1) * blocks)
        def _(j):
            for p in range(pairs):
                even = coup[j, pl.ds(p, listed, stride=width), :]
                odd = coup[j, pl.ds(p + pairs, listed, stride=width), :]
                high, low = split(jnp.concatenate([even, odd], axis=1))
                x_buf[j, p * listed : (p + 1) * listed, : 2 * rank] = high
                x_buf[j, p * listed : (p + 1) * listed, 2 * rank :] = low

    own_bases.wait()
    for copy in base_copies:
        copy.wait()
    for m in range(group):
        whole = bas[:, m].reshape(rank, bas.shape[-1])
        gram = dot_nt(whole, whole)
        grams[m] = gram
        gram_rows[pl.ds(m, rank, stride=BATCH), :] = gram
    factor_batch(rank, gram_rows, cols, upper)
    for m in range(group):
        low = upper[pl.ds(m, rank, stride=BATCH), :].T
        low_packed[q * group + m] = jnp.concatenate([low[:half], low[half:]], axis=1)
        low_own[m] = jnp.concatenate(
            [low[s * width + h * pairs : s * width + (h + 1) * pairs] for h in range(2) for s in range(n_rk)], axis=0
        )
    low_copies = [to_rk(low_packed.at[own_rows], low_packed.at[own_rows], low_s, low_r, d) for d in range(1, n_rk)]
    for copy in low_copies:
        copy.start()

    own_moves.wait()
    partial = jnp.zeros((rank, rank), F32)
    for m in range(group):
        partial = partial + dot_tn(moves[m], dot(grams[m], moves[m], HIGHEST))
    g1[q] = partial
    g1_copies = [to_rk(g1.at[q], g1.at[q], g1_s, g1_r, d) for d in range(1, n_rk)]
    for copy in g1_copies:
        copy.start()

    for copy in low_copies:
        copy.wait()
    lane = lax.broadcasted_iota(jnp.int32, (half, 2 * rank), 1)

    @pl.loop(0, leaves)
    def _(j):
        packed = low_packed[j]
        turned = pltpu.roll(packed, rank, 1)
        factor = jnp.concatenate(
            [
                jnp.where(lane < rank, packed, 0.0),
                jnp.where(lane < rank, turned, 0.0),
                jnp.where(lane >= rank, turned, 0.0),
                jnp.where(lane >= rank, packed, 0.0),
            ],
            axis=0,
        )
        high, low = split(factor)
        prod = dot(x_buf[j], jnp.concatenate([high, high], axis=0)) + dot(x_buf[j, :, : 2 * rank], low)
        high, low = split(prod)
        rows = pl.ds(pl.multiple_of(j * listed, listed), listed)
        for p in range(pairs):
            p_high[rows, p * 2 * rank : (p + 1) * 2 * rank] = high[p * listed : (p + 1) * listed]
            p_low[rows, p * 2 * rank : (p + 1) * 2 * rank] = low[p * listed : (p + 1) * listed]

    def clu_copy(c, d):
        return pltpu.make_async_remote_copy(
            src_ref=acc.at[c, clu_peer(d)],
            dst_ref=arrived.at[c, d],
            send_sem=rs_s.at[c, d],
            recv_sem=rs_r.at[c, d],
            device_id={"clu": clu_peer(d)},
            device_id_type=pl.DeviceIdType.MESH,
        )

    for c in range(CHUNKS):
        lanes = slice(c * part, (c + 1) * part)
        for first in range(0, n_clu, 8):
            size = min(8, n_clu - first)
            routes = onehot[first * leaves : (first + size) * leaves, :]
            total = dot(routes, p_high[:, lanes]) + dot(routes, p_low[:, lanes])
            acc[c, first : first + size] = total.reshape(size, leaves, part)
        for d in range(1, n_clu):
            clu_copy(c, d).start()

    start = lax.rem(q * width, half)
    held = low_packed[:, pl.ds(pl.multiple_of(start, width), width), :]
    held = jnp.where(q * width >= half, pltpu.roll(held, rank, 2), held)
    lw_ref[...] = held[:, :, :rank]

    for copy in g1_copies:
        copy.wait()
    level = g1[0]
    for s in range(1, n_rk):
        level = level + g1[s]
    levels = [level]
    for bit, transfer_ref in enumerate((node_ref, pair_ref, quad_ref)):
        transfer = transfer_ref[...]
        term = dot_tn(transfer, dot(level, transfer, HIGHEST))
        term_send[bit] = term
        mask = 2**bit
        partner = me + (1 - 2 * lax.rem(me // mask, 2)) * mask
        copy = pltpu.make_async_remote_copy(
            src_ref=term_send.at[bit],
            dst_ref=term_recv.at[bit],
            send_sem=lev_s.at[bit],
            recv_sem=lev_r.at[bit],
            device_id={"clu": partner},
            device_id_type=pl.DeviceIdType.MESH,
        )
        copy.start()
        copy.wait()
        level = term + term_recv[bit]
        levels.append(level)
    for m in range(BATCH):
        gram_rows[pl.ds(m, rank, stride=BATCH), :] = levels[m % len(levels)]
    factor_batch(rank, gram_rows, cols, upper)
    for m in range(len(levels)):
        low_node[m] = upper[pl.ds(m, rank, stride=BATCH), :].T
        nw_ref[m] = low_node[m, pl.ds(pl.multiple_of(q * width, width), width), :]

    for c in range(CHUNKS):
        total = acc[c, me]
        for d in range(1, n_clu):
            clu_copy(c, d).wait()
            total = total + arrived[c, d]
        per = part // (2 * rank)
        for s in range(per):
            mine[pl.ds(c * per + s, leaves, stride=pairs), :] = total[:, s * 2 * rank : (s + 1) * 2 * rank]
    share = group * pairs
    own = pl.ds(pl.multiple_of(q * share, share), share)
    mine_copies = [
        to_rk(
            mine.at[pl.ds(pl.multiple_of(rk_peer(d) * share, share), share)], theirs.at[q], mine_s, mine_r, d
        )
        for d in range(1, n_rk)
    ]
    for copy in mine_copies:
        copy.start()
    theirs[q] = mine[own, :]
    for copy in mine_copies:
        copy.wait()
    for m in range(group):
        gathered = theirs[:, m * pairs : (m + 1) * pairs, :].reshape(n_rk * pairs, 2 * rank)
        gathered = jnp.concatenate([gathered[:, :rank], gathered[:, rank:]], axis=0)
        coupled = dot_tn(gathered, low_own[m])
        for s in range(n_rk):
            out_send[s, m] = coupled[s * width : (s + 1) * width]
    out_copies = [to_rk(out_send.at[rk_peer(d)], out_recv.at[q], out_s, out_r, d) for d in range(1, n_rk)]
    for copy in out_copies:
        copy.start()
    out_recv[q] = out_send[q]
    for copy in out_copies:
        copy.wait()
    cp_ref[...] = out_recv[...].reshape(leaves, width, rank)


def shards(
    bases,
    leaf_transfer,
    node_transfer,
    pair_transfer,
    quad_transfer,
    coupling,
    row_device,
    row_slot,
    block_count,
):
    n_clu, n_rk = lax.axis_size("clu"), lax.axis_size("rk")
    _, leaves, points, width = bases.shape
    listed = coupling.shape[2]
    rank = width * n_rk
    group = leaves // n_rk
    pairs = width // 2
    count = leaves * listed
    feature = width * rank
    part = feature // CHUNKS
    valid = jnp.arange(listed, dtype=jnp.int32)[None, :] < block_count[0][:, None]
    target = jnp.where(valid, row_device[0, :, :, 0] * leaves + row_slot[0], -1).reshape(1, count)

    vmem = pl.BlockSpec(memory_space=pltpu.VMEM)
    hbm = pl.BlockSpec(memory_space=pl.ANY)
    dma = pltpu.SemaphoreType.DMA
    lw, nw, cp = pl.pallas_call(
        functools.partial(kernel, n_clu, n_rk, leaves, listed, width),
        out_shape=(
            jax.ShapeDtypeStruct((leaves, width, rank), F32),
            jax.ShapeDtypeStruct((4, width, rank), F32),
            jax.ShapeDtypeStruct((leaves, width, rank), F32),
        ),
        in_specs=[hbm, hbm, hbm, vmem, vmem, vmem, vmem],
        out_specs=(vmem, vmem, vmem),
        scratch_shapes=[
            pltpu.VMEM((n_rk, group, width, points), F32),
            pltpu.VMEM((leaves, listed * width, rank), F32),
            pltpu.VMEM((group, rank, rank), F32),
            pltpu.VMEM((leaves, listed * pairs, 4 * rank), BF16),
            pltpu.VMEM((n_clu * leaves, count), BF16),
            pltpu.VMEM((rank * BATCH, rank), F32),
            pltpu.VMEM((rank, rank, BATCH), F32),
            pltpu.VMEM((rank * BATCH, rank), F32),
            pltpu.VMEM((group, rank, rank), F32),
            pltpu.VMEM((leaves, rank // 2, 2 * rank), F32),
            pltpu.VMEM((group, rank, rank), F32),
            pltpu.VMEM((count, feature), BF16),
            pltpu.VMEM((count, feature), BF16),
            pltpu.VMEM((CHUNKS, n_clu, leaves, part), F32),
            pltpu.VMEM((CHUNKS, n_clu, leaves, part), F32),
            pltpu.VMEM((leaves * pairs, 2 * rank), F32),
            pltpu.VMEM((n_rk, group * pairs, 2 * rank), F32),
            pltpu.VMEM((n_rk, group, width, rank), F32),
            pltpu.VMEM((n_rk, group, width, rank), F32),
            pltpu.VMEM((n_rk, rank, rank), F32),
            pltpu.VMEM((3, rank, rank), F32),
            pltpu.VMEM((3, rank, rank), F32),
            pltpu.VMEM((4, rank, rank), F32),
            dma((CHUNKS + 2,)),
            dma((n_rk,)),
            dma((n_rk,)),
            dma((n_rk,)),
            dma((n_rk,)),
            dma((n_rk,)),
            dma((n_rk,)),
            dma((3,)),
            dma((3,)),
            dma((CHUNKS, n_clu)),
            dma((CHUNKS, n_clu)),
            dma((n_rk,)),
            dma((n_rk,)),
            dma((n_rk,)),
            dma((n_rk,)),
        ],
        compiler_params=pltpu.CompilerParams(
            collective_id=0, has_side_effects=True, vmem_limit_bytes=58 * 2**20
        ),
    )(
        jnp.swapaxes(bases[0], 1, 2),
        coupling[0].reshape(leaves, listed * width, rank),
        leaf_transfer[0],
        node_transfer[0],
        pair_transfer[0],
        quad_transfer[0],
        target,
    )
    return (
        jnp.swapaxes(lw, 1, 2)[None],
        jnp.swapaxes(nw, 1, 2)[:, None],
        jnp.swapaxes(cp, 1, 2)[None],
    )


def solution(mesh):
    placed = (
        P("clu", None, None, "rk"),
        P("clu", None, None, None),
        P("clu", None, None),
        P("clu", None, None),
        P("clu", None, None),
        P("clu", None, None, "rk", None),
        P("clu", None, None, None),
        P("clu", None, None),
        P("clu", None),
    )
    return jax.shard_map(
        shards,
        mesh=mesh,
        in_specs=placed,
        out_specs=(
            P("clu", None, None, "rk"),
            P(None, "clu", None, "rk"),
            P("clu", None, None, "rk"),
        ),
        check_vma=False,
    )
```

time: 511 us -> 83.6 us (0.16)
  other arithmetic: 234 us -> 2.1 us
  waiting for transfers between devices: 170 us -> 0 us
  Pallas kernels: 0 us -> 74.8 us
  local copies, waits for them, and re-layouts: 48.1 us -> 5.68 us
  matrix products: 25.1 us -> 0 us
  starting transfers between devices: 18.8 us -> 0 us
  between operations: 14.3 us -> 0.64 us
    another operation x6 -> x0, other arithmetic: 214 us -> none  [the longest x4 212 us: upper_factor(): return jnp.swapaxes(jnp.linalg.cholesky(gram), -1, -2)]
    all_to_all x2 -> x0, waiting for transfers between devices: 135 us -> none  [the longest x1 135 us: shards(): lax.all_to_all(buffer, 'clu', split_axis=0, concat_axis=0, tiled=True)]
    pallas_call x0 -> x1, Pallas kernels: none -> 74.8 us  [shards(): pl.pallas_call(functools.partial(kernel, n_clu, n_rk, leaves, listed, wid...]
    dot_general x11 -> x0, matrix products: 25.1 us -> none  [the longest x1 13.7 us: shards(): prod = jnp.einsum('jkab,jcb->jkac', blocks, leaf_factor, precision=highest)]
    reduce_scatter x1 -> x0, waiting for transfers between devices: 21.8 us -> none  [shards(): lax.psum_scatter(partial_sum, 'rk', scatter_dimension=2, tiled=True)]
    scatter-add x1 -> x0, other arithmetic: 14.7 us -> none  [shards(): jax.ops.segment_sum(arrived.reshape(-1, feature), owner_ids, num_segments...]
    scatter x2 -> x0, local copies, waits for them, and re-layouts: 13.2 us -> none  [the longest x1 8.85 us: shards(): jnp.zeros((n_clu * capacity + 1, feature), jnp.float32).at[target].set(flat)]
    all_to_all x2 -> x0, starting transfers between devices: 13.1 us -> none  [the longest x1 7.28 us: shards(): lax.all_to_all(labels, 'clu', split_axis=0, concat_axis=0, tiled=True)]
  transfers between devices with their start and end apart: 7 -> 0, of which waited for: 6 -> 0; matrix products, arithmetic and copies ran while one was open for 56% -> 0% of each run, Pallas kernels for 0% -> 0%
where the time goes in v1:
time: 83.6 us; the launch traced here: 83.2 us
  Pallas kernels  74.8 us (89%)
  local copies, waits for them, and re-layouts  5.68 us (7%)
  other arithmetic  2.1 us (3%)
    pallas_call x1, Pallas kernels, shards(): pl.pallas_call(functools.partial(kernel, n_clu, n_rk, leaves, listed, wid...  74.8 us
    unnamed x3, local copies, waits for them, and re-layouts  4.71 us

profile of v1, /device:TPU:0, one launch (start us, length us, event | category | flops | bytes accessed | tf_op | source)
XLA Modules:
  0.0 83.2 jit_solution(10816484200639627)
XLA Ops:
  0.6 0.8 squeeze.24
  1.4 0.7 iota_compare_fusion
  2.2 0.1 lt.29
  2.2 0.8 multiply_reduce_fusion
  3.0 0.1 mul.18
  3.1 0.6 add_select_fusion.target_ref
  3.7 74.8 %shard_map.112 = (f32[32,16,64]{2,1,0:T(8,128)}, f32[4,16,64]{2,1,0:T(8,128)}, f32[32,16,64]{2,1,0:T(8,128)}) custom-call(f32[32,16,256]{2,1,0:T(8,128)} %bitcast.22, f32[32,512,64]{2,1,0:T(8,128)} %bitcast.20, f32[32,64,64]{2,1,0:T(8,128)} %bitcast.21, f32[64,64]{1,0:T(8,128)} %bitcast.25, f32[64,64]{1,0:T(8,128)} %bitcast.26, f32[64,64]{1,0:T(8,128)} %bitcast.27, ...), custom_call_target="tpu_custom_call" | custom-call | tf_op jit(solution)/shard_map/pallas_call | solution.py:365
  78.5 1.7 %copy.16 = f32[1,32,64,16]{2,3,1,0:T(8,128)} copy(f32[1,32,64,16]{2,3,1,0:T(8,128)} %bitcast.24) | data formatting | bytes 262144
  80.1 1.4 %copy.17 = f32[4,1,64,16]{2,3,1,0:T(8,128)} copy(f32[4,1,64,16]{2,3,1,0:T(8,128)} %bitcast.28) | data formatting | bytes 32768
  81.5 1.7 %copy.18 = f32[1,32,64,16]{2,3,1,0:T(8,128)} copy(f32[1,32,64,16]{2,3,1,0:T(8,128)} %bitcast.23) | data formatting | bytes 262144

commit v2 on v1

v2 whole, which is shorter than its diff:
```python
import functools

import jax
import jax.numpy as jnp
from jax import lax
from jax.experimental import pallas as pl
from jax.experimental.pallas import tpu as pltpu
from jax.sharding import PartitionSpec as P

HIGHEST = lax.Precision.HIGHEST
F32 = jnp.float32
BF16 = jnp.bfloat16
LOADS = 4
BATCH = 8
ACROSS_FIRST = (0, 2)


def dot(a, b, precision=None):
    return jnp.dot(a, b, precision=precision, preferred_element_type=F32)


def dot_nt(a, b):
    return lax.dot_general(a, b, (((1,), (1,)), ((), ())), precision=HIGHEST, preferred_element_type=F32)


def dot_tn(a, b):
    return lax.dot_general(a, b, (((0,), (0,)), ((), ())), precision=HIGHEST, preferred_element_type=F32)


def split(x):
    high = x.astype(BF16)
    return high, (x - high.astype(F32)).astype(BF16)


def factor_batch(rank, gram_ref, cols, upper_ref, beside):
    @pl.loop(0, rank, unroll=8)
    def _(i):
        cols[i] = gram_ref[pl.ds(pl.multiple_of(i * BATCH, BATCH), BATCH), :].T

    step = 4
    for k0 in range(0, rank, step):
        r0 = k0 // 8 * 8

        def body(group, accs):
            accs = list(accs)
            for s in range(step):
                j = group * step + s
                col = cols[j, r0:, :]
                for t in range(step):
                    accs[t] = accs[t] - col * cols[j, k0 + t : k0 + t + 1, :]
            return tuple(accs)

        accs = tuple(cols[k0 + t, r0:, :] for t in range(step))
        accs = list(lax.fori_loop(0, k0 // step, body, accs))
        for t in range(step):
            at = k0 + t - r0
            col = accs[t] * lax.rsqrt(accs[t][at : at + 1, :])
            cols[k0 + t, r0:, :] = col
            for u in range(t + 1, step):
                to = k0 + u - r0
                accs[u] = accs[u] - col * col[to : to + 1, :]
        beside(k0 // step)

    lane = lax.broadcasted_iota(jnp.int32, (BATCH, rank), 1)

    @pl.loop(0, rank, unroll=8)
    def _(k):
        row = cols[k].T
        upper_ref[pl.ds(pl.multiple_of(k * BATCH, BATCH), BATCH), :] = jnp.where(lane >= k, row, 0.0)


def kernel(
    n_clu,
    n_rk,
    leaves,
    listed,
    width,
    bases_ref,
    coup_ref,
    leaf_move_ref,
    node_ref,
    pair_ref,
    quad_ref,
    device_ref,
    slot_ref,
    count_ref,
    lw_ref,
    nw_ref,
    cp_ref,
    bas,
    coup,
    moves,
    moved,
    x_buf,
    onehot,
    gram_rows,
    cols,
    upper,
    grams,
    low_packed,
    low_own,
    p_high,
    p_low,
    acc,
    mine,
    theirs,
    out_send,
    out_recv,
    g1,
    term_send,
    term_recv,
    low_node,
    local_sem,
    bas_s,
    bas_r,
    low_s,
    low_r,
    g1_s,
    g1_r,
    lev_s,
    lev_r,
    rs_s,
    rs_r,
    mine_s,
    mine_r,
    out_s,
    out_r,
    *arrived,
):
    rank = width * n_rk
    half = rank // 2
    group = leaves // n_rk
    pairs = width // 2
    count = leaves * listed
    lanes = 2 * rank
    q = lax.axis_index("rk")
    me = lax.axis_index("clu")

    def rk_peer(d):
        return lax.rem(q + d, n_rk)

    def other(index, bit):
        return index + (1 - 2 * lax.rem(index // 2**bit, 2)) * 2**bit

    def to_rk(src, dst, send, recv, d):
        return pltpu.make_async_remote_copy(
            src_ref=src,
            dst_ref=dst,
            send_sem=send.at[d],
            recv_sem=recv.at[d],
            device_id={"rk": rk_peer(d)},
            device_id_type=pl.DeviceIdType.MESH,
        )

    blocks = leaves // LOADS
    loads = []
    for c in range(LOADS):
        rows = pl.ds(c * blocks, blocks)
        loads.append(pltpu.make_async_copy(coup_ref.at[rows], coup.at[rows], local_sem.at[c]))
        loads[-1].start()
    own_rows = pl.ds(q * group, group)
    own_bases = pltpu.make_async_copy(bases_ref.at[own_rows], bas.at[q], local_sem.at[LOADS])
    own_bases.start()
    own_moves = pltpu.make_async_copy(leaf_move_ref.at[own_rows], moves, local_sem.at[LOADS + 1])
    own_moves.start()

    barrier = pltpu.get_barrier_semaphore()
    for d in range(1, n_rk):
        pl.semaphore_signal(barrier, inc=1, device_id={"rk": rk_peer(d)}, device_id_type=pl.DeviceIdType.MESH)
    bits = n_clu.bit_length() - 1
    for bit in range(bits):
        pl.semaphore_signal(barrier, inc=1, device_id={"clu": other(me, bit)}, device_id_type=pl.DeviceIdType.MESH)
    pl.semaphore_wait(barrier, n_rk - 1 + bits)

    base_copies = [
        to_rk(bases_ref.at[pl.ds(rk_peer(d) * group, group)], bas.at[q], bas_s, bas_r, d) for d in range(1, n_rk)
    ]
    for copy in base_copies:
        copy.start()

    entry = lax.broadcasted_iota(jnp.int32, (1, listed), 1)
    targets = []
    for j in range(leaves):
        target = device_ref[j] * leaves + slot_ref[j : j + 1, :]
        targets.append(jnp.where(entry < count_ref[:, j : j + 1], target, -1))
    block_rows = 8 * leaves
    per_tile = 128 // listed
    for tile in range(leaves // per_tile):
        target = jnp.concatenate(targets[tile * per_tile : (tile + 1) * per_tile], axis=1)
        for first in range(0, n_clu * leaves, block_rows):
            size = min(block_rows, n_clu * leaves - first)
            owner = lax.broadcasted_iota(jnp.int32, (size, 128), 0) + first
            hit = jnp.where(owner == target, 1.0, 0.0).astype(BF16)
            onehot[first : first + size, tile * 128 : (tile + 1) * 128] = hit

    for c in range(LOADS):
        loads[c].wait()

        @pl.loop(c * blocks, (c + 1) * blocks)
        def _(j):
            for p in range(pairs):
                even = coup[j, pl.ds(p, listed, stride=width), :]
                odd = coup[j, pl.ds(p + pairs, listed, stride=width), :]
                high, low = split(jnp.concatenate([even, odd], axis=1))
                x_buf[j, p * listed : (p + 1) * listed, : 2 * rank] = high
                x_buf[j, p * listed : (p + 1) * listed, 2 * rank :] = low

    own_bases.wait()
    for copy in base_copies:
        copy.wait()
    for m in range(group):
        whole = bas[:, m].reshape(rank, bas.shape[-1])
        gram = dot_nt(whole, whole)
        grams[m] = gram
        gram_rows[pl.ds(m, rank, stride=BATCH), :] = gram

    own_moves.wait()
    g1_copies = [to_rk(g1.at[q], g1.at[q], g1_s, g1_r, d) for d in range(1, n_rk)]

    def first_level(n):
        if n < group:
            moved[n] = dot(grams[n], moves[n], HIGHEST)
        if n == group:
            tall = (group * rank, rank)
            g1[q] = dot_tn(moves[...].reshape(tall), moved[...].reshape(tall))
            for copy in g1_copies:
                copy.start()

    factor_batch(rank, gram_rows, cols, upper, first_level)
    for m in range(group):
        low = upper[pl.ds(m, rank, stride=BATCH), :].T
        low_packed[q * group + m] = jnp.concatenate([low[:half], low[half:]], axis=1)
        low_own[m] = jnp.concatenate(
            [low[s * width + h * pairs : s * width + (h + 1) * pairs] for h in range(2) for s in range(n_rk)], axis=0
        )

    def low_copy(n, owner, bit):
        rows = pl.ds(owner * group, group)
        return pltpu.make_async_remote_copy(
            src_ref=low_packed.at[rows],
            dst_ref=low_packed.at[rows],
            send_sem=low_s.at[n],
            recv_sem=low_r.at[n],
            device_id={"rk": other(q, bit)},
            device_id_type=pl.DeviceIdType.MESH,
        )

    across, beside, onward = low_copy(0, q, 1), low_copy(1, q, 0), low_copy(2, other(q, 1), 0)
    across.start()
    beside.start()

    low_lane = lax.broadcasted_iota(jnp.int32, (half, lanes), 1)

    def multiply(owner):
        @pl.loop(0, group, unroll=4)
        def _(i):
            j = owner * group + i
            packed = low_packed[j]
            turned = pltpu.roll(packed, rank, 1)
            factor = jnp.concatenate(
                [
                    jnp.where(low_lane < rank, packed, 0.0),
                    jnp.where(low_lane < rank, turned, 0.0),
                    jnp.where(low_lane >= rank, turned, 0.0),
                    jnp.where(low_lane >= rank, packed, 0.0),
                ],
                axis=0,
            )
            high, low = split(factor)
            prod = dot(x_buf[j], jnp.concatenate([high, high], axis=0)) + dot(x_buf[j, :, :lanes], low)
            high, low = split(prod)
            rows = pl.ds(pl.multiple_of(j * listed, listed), listed)
            for p in range(pairs):
                p_high[rows, p * lanes : (p + 1) * lanes] = high[p * listed : (p + 1) * listed]
                p_low[rows, p * lanes : (p + 1) * lanes] = low[p * listed : (p + 1) * listed]

    def level_copy(bit):
        return pltpu.make_async_remote_copy(
            src_ref=term_send.at[bit],
            dst_ref=term_recv.at[bit],
            send_sem=lev_s.at[bit],
            recv_sem=lev_r.at[bit],
            device_id={"clu": other(me, bit)},
            device_id_type=pl.DeviceIdType.MESH,
        )

    levels = []

    def lift(bit):
        if bit == 0:
            for copy in g1_copies:
                copy.wait()
            level = g1[0]
            for s in range(1, n_rk):
                level = level + g1[s]
        else:
            level_copy(bit - 1).wait()
            level = term_send[bit - 1] + term_recv[bit - 1]
        levels.append(level)
        if bit < 3:
            transfer = (node_ref, pair_ref, quad_ref)[bit][...]
            term_send[bit] = dot_tn(transfer, dot(level, transfer, HIGHEST))
            level_copy(bit).start()

    lift(0)
    multiply(q)
    beside.wait()
    lift(1)
    multiply(other(q, 0))
    across.wait()
    onward.start()
    lift(2)
    multiply(other(q, 1))
    onward.wait()
    multiply(other(other(q, 1), 0))

    def order(c):
        return [*range(1, bits), 0] if c in ACROSS_FIRST else [*range(bits)]

    def place(c, r):
        at = 0
        for bit in order(c):
            at = 2 * at + r // 2**bit % 2
        return at

    def keep(c, step):
        return lax.rem(me // 2 ** order(c)[step], 2)

    def reduce_copy(c, step):
        size = n_clu >> (step + 1)
        held = acc if step == 0 else arrived[step - 1]
        return pltpu.make_async_remote_copy(
            src_ref=held.at[c, pl.ds((1 - keep(c, step)) * size, size)],
            dst_ref=arrived[step].at[c],
            send_sem=rs_s.at[c, step],
            recv_sem=rs_r.at[c, step],
            device_id={"clu": other(me, order(c)[step])},
            device_id_type=pl.DeviceIdType.MESH,
        )

    def advance(c, step):
        reduce_copy(c, step).wait()
        size = n_clu >> (step + 1)
        held = acc if step == 0 else arrived[step - 1]
        kept = keep(c, step) * size
        if step == bits - 1:
            total = arrived[step][c, 0] + held[c, kept]
            mine[pl.ds(c, leaves, stride=pairs), :] = total
            return
        now = size // 2
        first = (1 - keep(c, step + 1)) * now
        mover, stay = pl.ds(first, now), pl.ds(now - first, now)
        arrived[step][c, mover] = arrived[step][c, mover] + held[c, pl.ds(kept + first, now)]
        reduce_copy(c, step + 1).start()
        arrived[step][c, stay] = arrived[step][c, stay] + held[c, pl.ds(kept + now - first, now)]

    for c in range(0, pairs, 2):
        wide = slice(c * lanes, (c + 2) * lanes)
        for first in range(0, n_clu, 8):
            size = min(8, n_clu - first)
            routes = onehot[first * leaves : (first + size) * leaves, :]
            total = dot(routes, p_high[:, wide]) + dot(routes, p_low[:, wide])
            for r in range(size):
                rows = total[r * leaves : (r + 1) * leaves]
                for t in range(2):
                    acc[c + t, place(c + t, first + r)] = rows[:, t * lanes : (t + 1) * lanes]
        for t in range(2):
            reduce_copy(c + t, 0).start()

    start = lax.rem(q * width, half)
    held = low_packed[:, pl.ds(pl.multiple_of(start, width), width), :]
    held = jnp.where(q * width >= half, pltpu.roll(held, rank, 2), held)
    lw_ref[...] = held[:, :, :rank]

    lift(3)
    for m in range(BATCH):
        gram_rows[pl.ds(m, rank, stride=BATCH), :] = levels[m % len(levels)]
    lag = 2
    waves = pairs + lag * (bits - 1)

    def wave(t):
        for step in range(bits - 1, -1, -1):
            if 0 <= t - lag * step < pairs:
                advance(t - lag * step, step)

    def reduce_beside(n):
        if n < waves:
            wave(n)

    factor_batch(rank, gram_rows, cols, upper, reduce_beside)
    for t in range(rank // 4, waves):
        wave(t)
    for m in range(len(levels)):
        low_node[m] = upper[pl.ds(m, rank, stride=BATCH), :].T
        nw_ref[m] = low_node[m, pl.ds(pl.multiple_of(q * width, width), width), :]

    share = group * pairs
    own = pl.ds(pl.multiple_of(q * share, share), share)
    mine_copies = [
        to_rk(
            mine.at[pl.ds(pl.multiple_of(rk_peer(d) * share, share), share)], theirs.at[q], mine_s, mine_r, d
        )
        for d in range(1, n_rk)
    ]
    for copy in mine_copies:
        copy.start()
    theirs[q] = mine[own, :]
    for copy in mine_copies:
        copy.wait()
    for m in range(group):
        gathered = theirs[:, m * pairs : (m + 1) * pairs, :].reshape(n_rk * pairs, 2 * rank)
        gathered = jnp.concatenate([gathered[:, :rank], gathered[:, rank:]], axis=0)
        coupled = dot_tn(gathered, low_own[m])
        for s in range(n_rk):
            out_send[s, m] = coupled[s * width : (s + 1) * width]
    out_copies = [to_rk(out_send.at[rk_peer(d)], out_recv.at[q], out_s, out_r, d) for d in range(1, n_rk)]
    for copy in out_copies:
        copy.start()
    out_recv[q] = out_send[q]
    for copy in out_copies:
        copy.wait()
    cp_ref[...] = out_recv[...].reshape(leaves, width, rank)


def hand_over(a_ref, b_ref, c_ref, a_out, b_out, c_out, sem):
    copies = [
        pltpu.make_async_copy(src, dst, sem.at[n])
        for n, (src, dst) in enumerate(((a_ref, a_out), (b_ref, b_out), (c_ref, c_out)))
    ]
    for copy in copies:
        copy.start()
    for copy in copies:
        copy.wait()


def shards(
    bases,
    leaf_transfer,
    node_transfer,
    pair_transfer,
    quad_transfer,
    coupling,
    row_device,
    row_slot,
    block_count,
):
    n_clu, n_rk = lax.axis_size("clu"), lax.axis_size("rk")
    _, leaves, points, width = bases.shape
    listed = coupling.shape[2]
    rank = width * n_rk
    group = leaves // n_rk
    pairs = width // 2
    count = leaves * listed
    feature = width * rank
    bits = n_clu.bit_length() - 1

    vmem = pl.BlockSpec(memory_space=pltpu.VMEM)
    hbm = pl.BlockSpec(memory_space=pl.ANY)
    dma = pltpu.SemaphoreType.DMA
    lw, nw, cp = pl.pallas_call(
        functools.partial(kernel, n_clu, n_rk, leaves, listed, width),
        out_shape=(
            jax.ShapeDtypeStruct((leaves, width, rank), F32),
            jax.ShapeDtypeStruct((4, width, rank), F32),
            jax.ShapeDtypeStruct((leaves, width, rank), F32),
        ),
        in_specs=[hbm, hbm, hbm, vmem, vmem, vmem, vmem, vmem, vmem],
        out_specs=(vmem, vmem, vmem),
        scratch_shapes=[
            pltpu.VMEM((n_rk, group, width, points), F32),
            pltpu.VMEM((leaves, listed * width, rank), F32),
            pltpu.VMEM((group, rank, rank), F32),
            pltpu.VMEM((group, rank, rank), F32),
            pltpu.VMEM((leaves, listed * pairs, 4 * rank), BF16),
            pltpu.VMEM((n_clu * leaves, count), BF16),
            pltpu.VMEM((rank * BATCH, rank), F32),
            pltpu.VMEM((rank, rank, BATCH), F32),
            pltpu.VMEM((rank * BATCH, rank), F32),
            pltpu.VMEM((group, rank, rank), F32),
            pltpu.VMEM((leaves, rank // 2, 2 * rank), F32),
            pltpu.VMEM((group, rank, rank), F32),
            pltpu.VMEM((count, feature), BF16),
            pltpu.VMEM((count, feature), BF16),
            pltpu.VMEM((pairs, n_clu, leaves, 2 * rank), F32),
            pltpu.VMEM((leaves * pairs, 2 * rank), F32),
            pltpu.VMEM((n_rk, group * pairs, 2 * rank), F32),
            pltpu.VMEM((n_rk, group, width, rank), F32),
            pltpu.VMEM((n_rk, group, width, rank), F32),
            pltpu.VMEM((n_rk, rank, rank), F32),
            pltpu.VMEM((3, rank, rank), F32),
            pltpu.VMEM((3, rank, rank), F32),
            pltpu.VMEM((4, rank, rank), F32),
            dma((LOADS + 2,)),
            dma((n_rk,)),
            dma((n_rk,)),
            dma((n_rk,)),
            dma((n_rk,)),
            dma((n_rk,)),
            dma((n_rk,)),
            dma((3,)),
            dma((3,)),
            dma((pairs, bits)),
            dma((pairs, bits)),
            dma((n_rk,)),
            dma((n_rk,)),
            dma((n_rk,)),
            dma((n_rk,)),
            *[pltpu.VMEM((pairs, n_clu >> (step + 1), leaves, 2 * rank), F32) for step in range(bits)],
        ],
        compiler_params=pltpu.CompilerParams(
            collective_id=0, has_side_effects=True, vmem_limit_bytes=58 * 2**20
        ),
    )(
        jnp.swapaxes(bases[0], 1, 2),
        coupling[0].reshape(leaves, listed * width, rank),
        leaf_transfer[0],
        node_transfer[0],
        pair_transfer[0],
        quad_transfer[0],
        jnp.swapaxes(row_device[0], 1, 2),
        row_slot[0],
        block_count,
    )
    held = (lw, nw, cp)
    lw, nw, cp = pl.pallas_call(
        hand_over,
        out_shape=tuple(jax.ShapeDtypeStruct(x.shape, x.dtype) for x in held),
        in_specs=[hbm] * 3,
        out_specs=(hbm,) * 3,
        scratch_shapes=[dma((3,))],
    )(*held)
    return (
        jnp.swapaxes(lw, 1, 2)[None],
        jnp.swapaxes(nw, 1, 2)[:, None],
        jnp.swapaxes(cp, 1, 2)[None],
    )


def solution(mesh):
    placed = (
        P("clu", None, None, "rk"),
        P("clu", None, None, None),
        P("clu", None, None),
        P("clu", None, None),
        P("clu", None, None),
        P("clu", None, None, "rk", None),
        P("clu", None, None, None),
        P("clu", None, None),
        P("clu", None),
    )
    return jax.shard_map(
        shards,
        mesh=mesh,
        in_specs=placed,
        out_specs=(
            P("clu", None, None, "rk"),
            P(None, "clu", None, "rk"),
            P("clu", None, None, "rk"),
        ),
        check_vma=False,
    )
```

time: 83.6 us -> 80.4 us (0.962)
  local copies, waits for them, and re-layouts: 5.68 us -> 0 us
  Pallas kernels: 74.8 us -> 79.5 us
  other arithmetic: 2.1 us -> 0 us
    pallas_call x0 -> x1, Pallas kernels: none -> 18 us  [shards(): pl.pallas_call(hand_over, out_shape=tuple((jax.ShapeDtypeStruct(x.shape,...]
    pallas_call x1, Pallas kernels: 74.8 us -> 61.5 us  [shards(): pl.pallas_call(functools.partial(kernel, n_clu, n_rk, leaves, listed, wid...]
    unnamed x3 -> x0, local copies, waits for them, and re-layouts: 4.71 us -> none
where the time goes in v2:
time: 80.4 us; the launch traced here: 80.1 us
  Pallas kernels  79.5 us (99%)
    pallas_call x1, Pallas kernels, shards(): pl.pallas_call(functools.partial(kernel, n_clu, n_rk, leaves, listed, wid...  61.5 us
    pallas_call x1, Pallas kernels, shards(): pl.pallas_call(hand_over, out_shape=tuple((jax.ShapeDtypeStruct(x.shape,...  18 us

profile of v2, /device:TPU:0, one launch (start us, length us, event | category | flops | bytes accessed | tf_op | source)
XLA Modules:
  0.0 80.1 jit_solution(16526885576043876982)
XLA Ops:
  0.6 61.5 %shard_map.112 = (f32[32,16,64]{2,1,0:T(8,128)}, f32[4,16,64]{2,1,0:T(8,128)}, f32[32,16,64]{2,1,0:T(8,128)}) custom-call(f32[32,16,256]{2,1,0:T(8,128)} %bitcast.23, f32[32,512,64]{2,1,0:T(8,128)} %bitcast.21, f32[32,64,64]{2,1,0:T(8,128)} %bitcast.22, f32[64,64]{1,0:T(8,128)} %bitcast.24, f32[64,64]{1,0:T(8,128)} %bitcast.25, f32[64,64]{1,0:T(8,128)} %bitcast.26, ...), custom_call_target="tpu_custom_call" | custom-call | tf_op jit(solution)/shard_map/pallas_call | solution.py:460
  62.1 18.0 %shard_map.113 = (f32[32,16,64]{2,1,0:T(8,128)}, f32[4,16,64]{2,1,0:T(8,128)}, f32[32,16,64]{2,1,0:T(8,128)}) custom-call(f32[32,16,64]{2,1,0:T(8,128)} %get-tuple-element.9.a_ref, f32[4,16,64]{2,1,0:T(8,128)} %get-tuple-element.10.b_ref, f32[32,16,64]{2,1,0:T(8,128)} %get-tuple-element.11.c_ref), custom_call_target="tpu_custom_call" | custom-call | tf_op jit(solution)/shard_map/pallas_call | solution.py:525

commit v3 on v2

--- a/solution.py
+++ b/solution.py
@@ -32,41 +32,39 @@
     return high, (x - high.astype(F32)).astype(BF16)
 
 
-def factor_batch(rank, gram_ref, cols, upper_ref, beside):
-    @pl.loop(0, rank, unroll=8)
-    def _(i):
-        cols[i] = gram_ref[pl.ds(pl.multiple_of(i * BATCH, BATCH), BATCH), :].T
-
-    step = 4
+def factor_batch(rank, gram_ref, tiles, upper_ref, beside):
+    slots = 128 // BATCH
+    for g in range(rank // slots):
+        tiles[g] = gram_ref[g * 128 : (g + 1) * 128, :].T
+    slot = lax.broadcasted_iota(jnp.int32, (1, 128), 1) // BATCH
+    step = 8
     for k0 in range(0, rank, step):
-        r0 = k0 // 8 * 8
-
-        def body(group, accs):
-            accs = list(accs)
-            for s in range(step):
-                j = group * step + s
-                col = cols[j, r0:, :]
-                for t in range(step):
-                    accs[t] = accs[t] - col * cols[j, k0 + t : k0 + t + 1, :]
-            return tuple(accs)
-
-        accs = tuple(cols[k0 + t, r0:, :] for t in range(step))
-        accs = list(lax.fori_loop(0, k0 // step, body, accs))
+        g, s0 = k0 // slots, k0 % slots
+        tile = tiles[g, k0:, :]
+        done = [tiles[h, k0:, :] for h in range(g)]
+        if s0:
+            done.append(jnp.where(slot < s0, tile, 0.0))
+        accs = []
         for t in range(step):
-            at = k0 + t - r0
-            col = accs[t] * lax.rsqrt(accs[t][at : at + 1, :])
-            cols[k0 + t, r0:, :] = col
+            acc = jnp.where(slot == s0 + t, tile, 0.0)
+            for old in done:
+                acc = acc - old * old[t : t + 1, :]
+            shift = 64
+            while shift >= BATCH:
+                acc = acc + pltpu.roll(acc, shift, 1)
+                shift //= 2
+            accs.append(acc)
+        for t in range(step):
+            col = accs[t] * lax.rsqrt(accs[t][t : t + 1, :])
+            tile = jnp.where(slot == s0 + t, col, tile)
             for u in range(t + 1, step):
-                to = k0 + u - r0
-                accs[u] = accs[u] - col * col[to : to + 1, :]
+                accs[u] = accs[u] - col * col[u : u + 1, :]
+        tiles[g, k0:, :] = tile
         beside(k0 // step)
-
-    lane = lax.broadcasted_iota(jnp.int32, (BATCH, rank), 1)
-
-    @pl.loop(0, rank, unroll=8)
-    def _(k):
-        row = cols[k].T
-        upper_ref[pl.ds(pl.multiple_of(k * BATCH, BATCH), BATCH), :] = jnp.where(lane >= k, row, 0.0)
+    row = lax.broadcasted_iota(jnp.int32, (128, rank), 0) // BATCH
+    lane = lax.broadcasted_iota(jnp.int32, (128, rank), 1)
+    for g in range(rank // slots):
+        upper_ref[g * 128 : (g + 1) * 128, :] = jnp.where(lane >= row + g * slots, tiles[g].T, 0.0)
 
 
 def kernel(
@@ -139,6 +137,12 @@
     def rk_peer(d):
         return lax.rem(q + d, n_rk)
 
+    def packed_rows(x):
+        return jnp.concatenate([x[:half], x[half:]], axis=1)
+
+    def unpacked_rows(x):
+        return jnp.concatenate([x[:, :rank], x[:, rank:]], axis=0)
+
     def other(index, bit):
         return index + (1 - 2 * lax.rem(index // 2**bit, 2)) * 2**bit
 
@@ -193,17 +197,17 @@
             hit = jnp.where(owner == target, 1.0, 0.0).astype(BF16)
             onehot[first : first + size, tile * 128 : (tile + 1) * 128] = hit
 
-    for c in range(LOADS):
+    def prepare(j):
+        for p in range(pairs):
+            even = coup[j, pl.ds(p, listed, stride=width), :]
+            odd = coup[j, pl.ds(p + pairs, listed, stride=width), :]
+            high, low = split(jnp.concatenate([even, odd], axis=1))
+            x_buf[j, p * listed : (p + 1) * listed, :lanes] = high
+            x_buf[j, p * listed : (p + 1) * listed, lanes:] = low
+
+    for c in range(LOADS // 2):
         loads[c].wait()
-
-        @pl.loop(c * blocks, (c + 1) * blocks)
-        def _(j):
-            for p in range(pairs):
-                even = coup[j, pl.ds(p, listed, stride=width), :]
-                odd = coup[j, pl.ds(p + pairs, listed, stride=width), :]
-                high, low = split(jnp.concatenate([even, odd], axis=1))
-                x_buf[j, p * listed : (p + 1) * listed, : 2 * rank] = high
-                x_buf[j, p * listed : (p + 1) * listed, 2 * rank :] = low
+        pl.loop(c * blocks, (c + 1) * blocks)(prepare)
 
     own_bases.wait()
     for copy in base_copies:
@@ -218,18 +222,22 @@
     g1_copies = [to_rk(g1.at[q], g1.at[q], g1_s, g1_r, d) for d in range(1, n_rk)]
 
     def first_level(n):
-        if n < group:
-            moved[n] = dot(grams[n], moves[n], HIGHEST)
-        if n == group:
+        for m in range(2 * n, min(2 * n + 2, group)):
+            moved[m] = dot(grams[m], moves[m], HIGHEST)
+        if 2 * n == group:
             tall = (group * rank, rank)
-            g1[q] = dot_tn(moves[...].reshape(tall), moved[...].reshape(tall))
+            g1[q] = packed_rows(dot_tn(moves[...].reshape(tall), moved[...].reshape(tall)))
             for copy in g1_copies:
                 copy.start()
+        for j in range(leaves // 2 + n * leaves * 4 // rank, leaves // 2 + (n + 1) * leaves * 4 // rank):
+            if j % blocks == 0:
+                loads[j // blocks].wait()
+            prepare(j)
 
     factor_batch(rank, gram_rows, cols, upper, first_level)
     for m in range(group):
         low = upper[pl.ds(m, rank, stride=BATCH), :].T
-        low_packed[q * group + m] = jnp.concatenate([low[:half], low[half:]], axis=1)
+        low_packed[q * group + m] = packed_rows(low)
         low_own[m] = jnp.concatenate(
             [low[s * width + h * pairs : s * width + (h + 1) * pairs] for h in range(2) for s in range(n_rk)], axis=0
         )
@@ -296,10 +304,11 @@
         else:
             level_copy(bit - 1).wait()
             level = term_send[bit - 1] + term_recv[bit - 1]
+        level = unpacked_rows(level)
         levels.append(level)
         if bit < 3:
             transfer = (node_ref, pair_ref, quad_ref)[bit][...]
-            term_send[bit] = dot_tn(transfer, dot(level, transfer, HIGHEST))
+            term_send[bit] = packed_rows(dot_tn(transfer, dot(level, transfer, HIGHEST)))
             level_copy(bit).start()
 
     lift(0)
@@ -370,7 +379,9 @@
     start = lax.rem(q * width, half)
     held = low_packed[:, pl.ds(pl.multiple_of(start, width), width), :]
     held = jnp.where(q * width >= half, pltpu.roll(held, rank, 2), held)
-    lw_ref[...] = held[:, :, :rank]
+    mid = leaves // 2
+    held_lane = lax.broadcasted_iota(jnp.int32, (mid, width, lanes), 2)
+    lw_ref[...] = jnp.where(held_lane < rank, held[:mid], pltpu.roll(held[mid:], rank, 2))
 
     lift(3)
     for m in range(BATCH):
@@ -384,15 +395,15 @@
                 advance(t - lag * step, step)
 
     def reduce_beside(n):
-        if n < waves:
-            wave(n)
+        for t in range(n * waves * 8 // rank, (n + 1) * waves * 8 // rank):
+            wave(t)
 
     factor_batch(rank, gram_rows, cols, upper, reduce_beside)
-    for t in range(rank // 4, waves):
-        wave(t)
     for m in range(len(levels)):
         low_node[m] = upper[pl.ds(m, rank, stride=BATCH), :].T
-        nw_ref[m] = low_node[m, pl.ds(pl.multiple_of(q * width, width), width), :]
+    ours = pl.ds(pl.multiple_of(q * width, width), width)
+    for m in range(2):
+        nw_ref[m] = jnp.concatenate([low_node[m, ours, :], low_node[m + 2, ours, :]], axis=1)
 
     share = group * pairs
     own = pl.ds(pl.multiple_of(q * share, share), share)
@@ -407,10 +418,12 @@
     theirs[q] = mine[own, :]
     for copy in mine_copies:
         copy.wait()
-    for m in range(group):
-        gathered = theirs[:, m * pairs : (m + 1) * pairs, :].reshape(n_rk * pairs, 2 * rank)
-        gathered = jnp.concatenate([gathered[:, :rank], gathered[:, rank:]], axis=0)
-        coupled = dot_tn(gathered, low_own[m])
+    for m in range(group // 2):
+        sums = []
+        for n in (m, m + group // 2):
+            gathered = theirs[:, n * pairs : (n + 1) * pairs, :].reshape(n_rk * pairs, lanes)
+            sums.append(dot_tn(unpacked_rows(gathered), low_own[n]))
+        coupled = jnp.concatenate(sums, axis=1)
         for s in range(n_rk):
             out_send[s, m] = coupled[s * width : (s + 1) * width]
     out_copies = [to_rk(out_send.at[rk_peer(d)], out_recv.at[q], out_s, out_r, d) for d in range(1, n_rk)]
@@ -419,18 +432,18 @@
     out_recv[q] = out_send[q]
     for copy in out_copies:
         copy.wait()
-    cp_ref[...] = out_recv[...].reshape(leaves, width, rank)
-
-
-def hand_over(a_ref, b_ref, c_ref, a_out, b_out, c_out, sem):
-    copies = [
-        pltpu.make_async_copy(src, dst, sem.at[n])
-        for n, (src, dst) in enumerate(((a_ref, a_out), (b_ref, b_out), (c_ref, c_out)))
-    ]
-    for copy in copies:
-        copy.start()
-    for copy in copies:
-        copy.wait()
+    cp_ref[...] = out_recv[...].reshape(leaves // 2, width, lanes)
+
+
+def unpack(group, lw_ref, nw_ref, cp_ref, lw_out, nw_out, cp_out):
+    for src, dst, run in ((lw_ref, lw_out, None), (nw_ref, nw_out, None), (cp_ref, cp_out, group)):
+        rank = dst.shape[2]
+        run = run or dst.shape[0]
+        half = run // 2
+        for n in range(0, dst.shape[0], run):
+            both = src[n // 2 : n // 2 + half]
+            dst[n : n + half] = both[:, :, :rank]
+            dst[n + half : n + run] = both[:, :, rank:]
 
 
 def shards(
@@ -460,9 +473,9 @@
     lw, nw, cp = pl.pallas_call(
         functools.partial(kernel, n_clu, n_rk, leaves, listed, width),
         out_shape=(
-            jax.ShapeDtypeStruct((leaves, width, rank), F32),
-            jax.ShapeDtypeStruct((4, width, rank), F32),
-            jax.ShapeDtypeStruct((leaves, width, rank), F32),
+            jax.ShapeDtypeStruct((leaves // 2, width, 2 * rank), F32),
+            jax.ShapeDtypeStruct((2, width, 2 * rank), F32),
+            jax.ShapeDtypeStruct((leaves // 2, width, 2 * rank), F32),
         ),
         in_specs=[hbm, hbm, hbm, vmem, vmem, vmem, vmem, vmem, vmem],
         out_specs=(vmem, vmem, vmem),
@@ -474,7 +487,7 @@
             pltpu.VMEM((leaves, listed * pairs, 4 * rank), BF16),
             pltpu.VMEM((n_clu * leaves, count), BF16),
             pltpu.VMEM((rank * BATCH, rank), F32),
-            pltpu.VMEM((rank, rank, BATCH), F32),
+            pltpu.VMEM((rank * BATCH // 128, rank, 128), F32),
             pltpu.VMEM((rank * BATCH, rank), F32),
             pltpu.VMEM((group, rank, rank), F32),
             pltpu.VMEM((leaves, rank // 2, 2 * rank), F32),
@@ -484,11 +497,11 @@
             pltpu.VMEM((pairs, n_clu, leaves, 2 * rank), F32),
             pltpu.VMEM((leaves * pairs, 2 * rank), F32),
             pltpu.VMEM((n_rk, group * pairs, 2 * rank), F32),
-            pltpu.VMEM((n_rk, group, width, rank), F32),
-            pltpu.VMEM((n_rk, group, width, rank), F32),
-            pltpu.VMEM((n_rk, rank, rank), F32),
-            pltpu.VMEM((3, rank, rank), F32),
-            pltpu.VMEM((3, rank, rank), F32),
+            pltpu.VMEM((n_rk, group // 2, width, 2 * rank), F32),
+            pltpu.VMEM((n_rk, group // 2, width, 2 * rank), F32),
+            pltpu.VMEM((n_rk, rank // 2, 2 * rank), F32),
+            pltpu.VMEM((3, rank // 2, 2 * rank), F32),
+            pltpu.VMEM((3, rank // 2, 2 * rank), F32),
             pltpu.VMEM((4, rank, rank), F32),
             dma((LOADS + 2,)),
             dma((n_rk,)),
@@ -521,14 +534,12 @@
         row_slot[0],
         block_count,
     )
-    held = (lw, nw, cp)
     lw, nw, cp = pl.pallas_call(
-        hand_over,
-        out_shape=tuple(jax.ShapeDtypeStruct(x.shape, x.dtype) for x in held),
-        in_specs=[hbm] * 3,
-        out_specs=(hbm,) * 3,
-        scratch_shapes=[dma((3,))],
-    )(*held)
+        functools.partial(unpack, leaves // n_rk),
+        out_shape=tuple(jax.ShapeDtypeStruct((2 * x.shape[0], width, rank), F32) for x in (lw, nw, cp)),
+        in_specs=[vmem] * 3,
+        out_specs=(vmem,) * 3,
+    )(lw, nw, cp)
     return (
         jnp.swapaxes(lw, 1, 2)[None],
         jnp.swapaxes(nw, 1, 2)[:, None],

time: 80.4 us -> 61.1 us (0.76)
  Pallas kernels: 79.5 us -> 60.3 us
    pallas_call x1, Pallas kernels: 18 us -> 1.89 us  [shards(): pl.pallas_call(functools.partial(unpack, leaves // n_rk), out_shape=tuple...]
    pallas_call x1, Pallas kernels: 61.5 us -> 58.4 us  [shards(): pl.pallas_call(functools.partial(kernel, n_clu, n_rk, leaves, listed, wid...]
where the time goes in v3:
time: 61.1 us; the launch traced here: 60.9 us
  Pallas kernels  60.3 us (99%)
  between operations  0.64 us (1%)
    pallas_call x1, Pallas kernels, shards(): pl.pallas_call(functools.partial(kernel, n_clu, n_rk, leaves, listed, wid...  58.4 us
    pallas_call x1, Pallas kernels, shards(): pl.pallas_call(functools.partial(unpack, leaves // n_rk), out_shape=tuple...  1.89 us

profile of v3, /device:TPU:0, one launch (start us, length us, event | category | flops | bytes accessed | tf_op | source)
XLA Modules:
  0.0 60.9 jit_solution(1989535768314447431)
XLA Ops:
  0.6 58.4 %shard_map.112 = (f32[16,16,128]{2,1,0:T(8,128)}, f32[2,16,128]{2,1,0:T(8,128)}, f32[16,16,128]{2,1,0:T(8,128)}) custom-call(f32[32,16,256]{2,1,0:T(8,128)} %bitcast.23, f32[32,512,64]{2,1,0:T(8,128)} %bitcast.21, f32[32,64,64]{2,1,0:T(8,128)} %bitcast.22, f32[64,64]{1,0:T(8,128)} %bitcast.24, f32[64,64]{1,0:T(8,128)} %bitcast.25, f32[64,64]{1,0:T(8,128)} %bitcast.26, ...), custom_call_target="tpu_custom_call" | custom-call | tf_op jit(solution)/shard_map/pallas_call | solution.py:473
  59.0 1.9 %shard_map.113 = (f32[32,16,64]{2,1,0:T(8,128)}, f32[4,16,64]{2,1,0:T(8,128)}, f32[32,16,64]{2,1,0:T(8,128)}) custom-call(f32[16,16,128]{2,1,0:T(8,128)} %get-tuple-element.9.lw_ref, f32[2,16,128]{2,1,0:T(8,128)} %get-tuple-element.10.nw_ref, f32[16,16,128]{2,1,0:T(8,128)} %get-tuple-element.11.cp_ref), custom_call_target="tpu_custom_call" | custom-call | tf_op jit(solution)/shard_map/pallas_call | solution.py:537

commit v4 on v3

--- a/solution.py
+++ b/solution.py
@@ -96,14 +96,12 @@
     upper,
     grams,
     low_packed,
-    low_own,
     p_high,
     p_low,
     acc,
-    mine,
+    packs,
     theirs,
-    out_send,
-    out_recv,
+    low_cat,
     g1,
     term_send,
     term_recv,
@@ -119,10 +117,8 @@
     lev_r,
     rs_s,
     rs_r,
-    mine_s,
-    mine_r,
-    out_s,
-    out_r,
+    give_s,
+    give_r,
     *arrived,
 ):
     rank = width * n_rk
@@ -205,7 +201,8 @@
             x_buf[j, p * listed : (p + 1) * listed, :lanes] = high
             x_buf[j, p * listed : (p + 1) * listed, lanes:] = low
 
-    for c in range(LOADS // 2):
+    early = LOADS - 1
+    for c in range(early):
         loads[c].wait()
         pl.loop(c * blocks, (c + 1) * blocks)(prepare)
 
@@ -229,7 +226,7 @@
             g1[q] = packed_rows(dot_tn(moves[...].reshape(tall), moved[...].reshape(tall)))
             for copy in g1_copies:
                 copy.start()
-        for j in range(leaves // 2 + n * leaves * 4 // rank, leaves // 2 + (n + 1) * leaves * 4 // rank):
+        for j in range(early * blocks + n * blocks * 8 // rank, early * blocks + (n + 1) * blocks * 8 // rank):
             if j % blocks == 0:
                 loads[j // blocks].wait()
             prepare(j)
@@ -238,9 +235,6 @@
     for m in range(group):
         low = upper[pl.ds(m, rank, stride=BATCH), :].T
         low_packed[q * group + m] = packed_rows(low)
-        low_own[m] = jnp.concatenate(
-            [low[s * width + h * pairs : s * width + (h + 1) * pairs] for h in range(2) for s in range(n_rk)], axis=0
-        )
 
     def low_copy(n, owner, bit):
         rows = pl.ds(owner * group, group)
@@ -313,11 +307,11 @@
 
     lift(0)
     multiply(q)
-    beside.wait()
-    lift(1)
-    multiply(other(q, 0))
     across.wait()
     onward.start()
+    lift(1)
+    beside.wait()
+    multiply(other(q, 0))
     lift(2)
     multiply(other(q, 1))
     onward.wait()
@@ -347,6 +341,14 @@
             device_id_type=pl.DeviceIdType.MESH,
         )
 
+    give_lane = lax.broadcasted_iota(jnp.int32, (8, lanes), 1) // width
+
+    def give_rows(c):
+        return pl.ds(pl.multiple_of((q * pairs + c) * 8, 8), 8)
+
+    def give_copy(c, d):
+        return to_rk(packs.at[c, rk_peer(d)], theirs.at[give_rows(c)], give_s.at[c], give_r.at[c], d)
+
     def advance(c, step):
         reduce_copy(c, step).wait()
         size = n_clu >> (step + 1)
@@ -354,7 +356,19 @@
         kept = keep(c, step) * size
         if step == bits - 1:
             total = arrived[step][c, 0] + held[c, kept]
-            mine[pl.ds(c, leaves, stride=pairs), :] = total
+            for dest in range(n_rk):
+                out = jnp.zeros((8, lanes), F32)
+                for g in range(leaves // 8):
+                    for par in range(2):
+                        to = (2 * g + par) * width
+                        shift = (to - par * rank - dest * width) % lanes
+                        piece = total[8 * g : 8 * g + 8]
+                        piece = pltpu.roll(piece, shift, 1) if shift else piece
+                        out = jnp.where(give_lane == 2 * g + par, piece, out)
+                packs[c, dest] = out
+            for d in range(1, n_rk):
+                give_copy(c, d).start()
+            theirs[give_rows(c), :] = packs[c, q]
             return
         now = size // 2
         first = (1 - keep(c, step + 1)) * now
@@ -376,6 +390,25 @@
         for t in range(2):
             reduce_copy(c + t, 0).start()
 
+    cat_lane = lax.broadcasted_iota(jnp.int32, (width, lanes), 1) < rank
+    for n in range(leaves):
+        g, low = n // 8, n % 8
+        packed = low_packed[n]
+        turned = pltpu.roll(packed, rank, 1)
+
+        def rows_of(x, par):
+            return jnp.concatenate([x[8 * par : 8 * par + 8], x[width + 8 * par : width + 8 * par + 8]], axis=0)
+
+        both = jnp.concatenate(
+            [
+                jnp.where(cat_lane, rows_of(packed, 0), rows_of(turned, 1)),
+                jnp.where(cat_lane, rows_of(turned, 0), rows_of(packed, 1)),
+            ],
+            axis=0,
+        )
+        high, rest = split(both)
+        low_cat[low, :, g * lanes : (g + 1) * lanes] = jnp.concatenate([high, rest, high], axis=0)
+
     start = lax.rem(q * width, half)
     held = low_packed[:, pl.ds(pl.multiple_of(start, width), width), :]
     held = jnp.where(q * width >= half, pltpu.roll(held, rank, 2), held)
@@ -405,45 +438,31 @@
     for m in range(2):
         nw_ref[m] = jnp.concatenate([low_node[m, ours, :], low_node[m + 2, ours, :]], axis=1)
 
-    share = group * pairs
-    own = pl.ds(pl.multiple_of(q * share, share), share)
-    mine_copies = [
-        to_rk(
-            mine.at[pl.ds(pl.multiple_of(rk_peer(d) * share, share), share)], theirs.at[q], mine_s, mine_r, d
-        )
-        for d in range(1, n_rk)
-    ]
-    for copy in mine_copies:
-        copy.start()
-    theirs[q] = mine[own, :]
-    for copy in mine_copies:
-        copy.wait()
-    for m in range(group // 2):
-        sums = []
-        for n in (m, m + group // 2):
-            gathered = theirs[:, n * pairs : (n + 1) * pairs, :].reshape(n_rk * pairs, lanes)
-            sums.append(dot_tn(unpacked_rows(gathered), low_own[n]))
-        coupled = jnp.concatenate(sums, axis=1)
-        for s in range(n_rk):
-            out_send[s, m] = coupled[s * width : (s + 1) * width]
-    out_copies = [to_rk(out_send.at[rk_peer(d)], out_recv.at[q], out_s, out_r, d) for d in range(1, n_rk)]
-    for copy in out_copies:
-        copy.start()
-    out_recv[q] = out_send[q]
-    for copy in out_copies:
-        copy.wait()
-    cp_ref[...] = out_recv[...].reshape(leaves // 2, width, lanes)
-
-
-def unpack(group, lw_ref, nw_ref, cp_ref, lw_out, nw_out, cp_out):
-    for src, dst, run in ((lw_ref, lw_out, None), (nw_ref, nw_out, None), (cp_ref, cp_out, group)):
-        rank = dst.shape[2]
-        run = run or dst.shape[0]
-        half = run // 2
-        for n in range(0, dst.shape[0], run):
-            both = src[n // 2 : n // 2 + half]
-            dst[n : n + half] = both[:, :, :rank]
-            dst[n + half : n + run] = both[:, :, rank:]
+    for c in range(pairs):
+        for d in range(1, n_rk):
+            give_copy(c, d).wait()
+    for n in range(8):
+        high, low = split(theirs[pl.ds(n, n_rk * pairs, stride=8), :])
+        tall = jnp.concatenate([high, high, low], axis=0)
+        out = lax.dot_general(tall, low_cat[n], (((0,), (0,)), ((), ())), preferred_element_type=F32)
+        blocks_of = []
+        for g in range(leaves // 8):
+            block = out[2 * g * width : 2 * (g + 1) * width, g * lanes : (g + 1) * lanes]
+            blocks_of.append((block[:width], block[width:]))
+        for g in range(leaves // 16):
+            even, odd = blocks_of[g]
+            left = even + pltpu.roll(odd, rank, 1)
+            even, odd = blocks_of[g + leaves // 16]
+            right = pltpu.roll(even, rank, 1) + odd
+            cp_ref[8 * g + n] = jnp.where(cat_lane, left, right)
+
+
+def unpack(lw_ref, nw_ref, cp_ref, lw_out, nw_out, cp_out):
+    for src, dst in ((lw_ref, lw_out), (nw_ref, nw_out), (cp_ref, cp_out)):
+        rank, half = dst.shape[2], src.shape[0]
+        both = src[...]
+        dst[:half] = both[:, :, :rank]
+        dst[half:] = both[:, :, rank:]
 
 
 def shards(
@@ -491,14 +510,12 @@
             pltpu.VMEM((rank * BATCH, rank), F32),
             pltpu.VMEM((group, rank, rank), F32),
             pltpu.VMEM((leaves, rank // 2, 2 * rank), F32),
-            pltpu.VMEM((group, rank, rank), F32),
             pltpu.VMEM((count, feature), BF16),
             pltpu.VMEM((count, feature), BF16),
             pltpu.VMEM((pairs, n_clu, leaves, 2 * rank), F32),
-            pltpu.VMEM((leaves * pairs, 2 * rank), F32),
-            pltpu.VMEM((n_rk, group * pairs, 2 * rank), F32),
-            pltpu.VMEM((n_rk, group // 2, width, 2 * rank), F32),
-            pltpu.VMEM((n_rk, group // 2, width, 2 * rank), F32),
+            pltpu.VMEM((pairs, n_rk, 8, 2 * rank), F32),
+            pltpu.VMEM((n_rk * pairs * 8, 2 * rank), F32),
+            pltpu.VMEM((8, 6 * width, leaves // 4 * rank), BF16),
             pltpu.VMEM((n_rk, rank // 2, 2 * rank), F32),
             pltpu.VMEM((3, rank // 2, 2 * rank), F32),
             pltpu.VMEM((3, rank // 2, 2 * rank), F32),
@@ -514,10 +531,8 @@
             dma((3,)),
             dma((pairs, bits)),
             dma((pairs, bits)),
-            dma((n_rk,)),
-            dma((n_rk,)),
-            dma((n_rk,)),
-            dma((n_rk,)),
+            dma((pairs, n_rk)),
+            dma((pairs, n_rk)),
             *[pltpu.VMEM((pairs, n_clu >> (step + 1), leaves, 2 * rank), F32) for step in range(bits)],
         ],
         compiler_params=pltpu.CompilerParams(
@@ -535,7 +550,7 @@
         block_count,
     )
     lw, nw, cp = pl.pallas_call(
-        functools.partial(unpack, leaves // n_rk),
+        unpack,
         out_shape=tuple(jax.ShapeDtypeStruct((2 * x.shape[0], width, rank), F32) for x in (lw, nw, cp)),
         in_specs=[vmem] * 3,
         out_specs=(vmem,) * 3,

time: 61.1 us -> 57.4 us (0.939)
  Pallas kernels: 60.3 us -> 56.6 us
    pallas_call x1, Pallas kernels: 58.4 us -> 54.7 us  [shards(): pl.pallas_call(functools.partial(kernel, n_clu, n_rk, leaves, listed, wid...]
where the time goes in v4:
time: 57.4 us; the launch traced here: 57.2 us
  Pallas kernels  56.6 us (99%)
  between operations  0.64 us (1%)
    pallas_call x1, Pallas kernels, shards(): pl.pallas_call(functools.partial(kernel, n_clu, n_rk, leaves, listed, wid...  54.7 us
    pallas_call x1, Pallas kernels, shards(): pl.pallas_call(unpack, out_shape=tuple((jax.ShapeDtypeStruct((2 * x.shape...  1.89 us

profile of v4, /device:TPU:0, one launch (start us, length us, event | category | flops | bytes accessed | tf_op | source)
XLA Modules:
  0.0 57.2 jit_solution(15484265828113745860)
XLA Ops:
  0.6 54.7 %shard_map.112 = (f32[16,16,128]{2,1,0:T(8,128)}, f32[2,16,128]{2,1,0:T(8,128)}, f32[16,16,128]{2,1,0:T(8,128)}) custom-call(f32[32,16,256]{2,1,0:T(8,128)} %bitcast.23, f32[32,512,64]{2,1,0:T(8,128)} %bitcast.21, f32[32,64,64]{2,1,0:T(8,128)} %bitcast.22, f32[64,64]{1,0:T(8,128)} %bitcast.24, f32[64,64]{1,0:T(8,128)} %bitcast.25, f32[64,64]{1,0:T(8,128)} %bitcast.26, ...), custom_call_target="tpu_custom_call" | custom-call | tf_op jit(solution)/shard_map/pallas_call | solution.py:492
  55.4 1.9 %shard_map.113 = (f32[32,16,64]{2,1,0:T(8,128)}, f32[4,16,64]{2,1,0:T(8,128)}, f32[32,16,64]{2,1,0:T(8,128)}) custom-call(f32[16,16,128]{2,1,0:T(8,128)} %get-tuple-element.9.lw_ref, f32[2,16,128]{2,1,0:T(8,128)} %get-tuple-element.10.nw_ref, f32[16,16,128]{2,1,0:T(8,128)} %get-tuple-element.11.cp_ref), custom_call_target="tpu_custom_call" | custom-call | tf_op jit(solution)/shard_map/pallas_call | solution.py:552

commit v5 on v4

--- a/solution.py
+++ b/solution.py
@@ -54,11 +54,26 @@
                 acc = acc + pltpu.roll(acc, shift, 1)
                 shift //= 2
             accs.append(acc)
+        corner = {}
         for t in range(step):
-            col = accs[t] * lax.rsqrt(accs[t][t : t + 1, :])
-            tile = jnp.where(slot == s0 + t, col, tile)
+            for u in range(t, step):
+                corner[u, t] = jnp.broadcast_to(accs[t][u : u + 1, :], (step, 128))
+        inverse = []
+        for t in range(step):
+            inverse.append(lax.rsqrt(corner[t, t]))
             for u in range(t + 1, step):
-                accs[u] = accs[u] - col * col[u : u + 1, :]
+                corner[u, t] = corner[u, t] * inverse[t]
+            for u in range(t + 1, step):
+                for v in range(t + 1, u + 1):
+                    corner[u, v] = corner[u, v] - corner[u, t] * corner[v, t]
+        deep = (rank - k0) // step, step, 128
+        columns = []
+        for t in range(step):
+            col = accs[t].reshape(deep)
+            for v in range(t):
+                col = col - columns[v] * corner[t, v][None]
+            columns.append(col * inverse[t][None])
+            tile = jnp.where(slot == s0 + t, columns[t].reshape(tile.shape), tile)
         tiles[g, k0:, :] = tile
         beside(k0 // step)
     row = lax.broadcasted_iota(jnp.int32, (128, rank), 0) // BATCH
@@ -254,8 +269,7 @@
     low_lane = lax.broadcasted_iota(jnp.int32, (half, lanes), 1)
 
     def multiply(owner):
-        @pl.loop(0, group, unroll=4)
-        def _(i):
+        for i in range(group):
             j = owner * group + i
             packed = low_packed[j]
             turned = pltpu.roll(packed, rank, 1)
@@ -303,17 +317,17 @@
         if bit < 3:
             transfer = (node_ref, pair_ref, quad_ref)[bit][...]
             term_send[bit] = packed_rows(dot_tn(transfer, dot(level, transfer, HIGHEST)))
-            level_copy(bit).start()
 
     lift(0)
     multiply(q)
+    level_copy(0).start()
+    beside.wait()
+    multiply(other(q, 0))
     across.wait()
     onward.start()
     lift(1)
-    beside.wait()
-    multiply(other(q, 0))
-    lift(2)
     multiply(other(q, 1))
+    level_copy(1).start()
     onward.wait()
     multiply(other(other(q, 1), 0))
 
@@ -377,7 +391,16 @@
         reduce_copy(c, step + 1).start()
         arrived[step][c, stay] = arrived[step][c, stay] + held[c, pl.ds(kept + now - first, now)]
 
+    lag = 2
+
+    def wave(t):
+        for step in range(bits - 1, -1, -1):
+            if 0 <= t - lag * step < pairs:
+                advance(t - lag * step, step)
+
     for c in range(0, pairs, 2):
+        if c == 2:
+            lift(2)
         wide = slice(c * lanes, (c + 2) * lanes)
         for first in range(0, n_clu, 8):
             size = min(8, n_clu - first)
@@ -389,6 +412,10 @@
                     acc[c + t, place(c + t, first + r)] = rows[:, t * lanes : (t + 1) * lanes]
         for t in range(2):
             reduce_copy(c + t, 0).start()
+        if c == 2:
+            level_copy(2).start()
+        if c >= 4:
+            wave((c - 4) // 2)
 
     cat_lane = lax.broadcasted_iota(jnp.int32, (width, lanes), 1) < rank
     for n in range(leaves):
@@ -416,20 +443,16 @@
     held_lane = lax.broadcasted_iota(jnp.int32, (mid, width, lanes), 2)
     lw_ref[...] = jnp.where(held_lane < rank, held[:mid], pltpu.roll(held[mid:], rank, 2))
 
+    wave(2)
     lift(3)
     for m in range(BATCH):
         gram_rows[pl.ds(m, rank, stride=BATCH), :] = levels[m % len(levels)]
-    lag = 2
-    waves = pairs + lag * (bits - 1)
-
-    def wave(t):
-        for step in range(bits - 1, -1, -1):
-            if 0 <= t - lag * step < pairs:
-                advance(t - lag * step, step)
+    wave(3)
+    waves = pairs + lag * (bits - 1) - 4
 
     def reduce_beside(n):
         for t in range(n * waves * 8 // rank, (n + 1) * waves * 8 // rank):
-            wave(t)
+            wave(4 + t)
 
     factor_batch(rank, gram_rows, cols, upper, reduce_beside)
     for m in range(len(levels)):

time: 57.4 us -> 56.8 us (0.990)
  Pallas kernels: 56.6 us -> 55.9 us
    pallas_call x1, Pallas kernels: 54.7 us -> 54 us  [shards(): pl.pallas_call(functools.partial(kernel, n_clu, n_rk, leaves, listed, wid...]
where the time goes in v5:
time: 56.8 us; the launch traced here: 56.6 us
  Pallas kernels  55.9 us (98%)
  between operations  0.64 us (1%)
    pallas_call x1, Pallas kernels, shards(): pl.pallas_call(functools.partial(kernel, n_clu, n_rk, leaves, listed, wid...  54 us
    pallas_call x1, Pallas kernels, shards(): pl.pallas_call(unpack, out_shape=tuple((jax.ShapeDtypeStruct((2 * x.shape...  1.89 us

profile of v5, /device:TPU:0, one launch (start us, length us, event | category | flops | bytes accessed | tf_op | source)
XLA Modules:
  0.0 56.6 jit_solution(6362355735724969558)
XLA Ops:
  0.6 54.0 %shard_map.112 = (f32[16,16,128]{2,1,0:T(8,128)}, f32[2,16,128]{2,1,0:T(8,128)}, f32[16,16,128]{2,1,0:T(8,128)}) custom-call(f32[32,16,256]{2,1,0:T(8,128)} %bitcast.23, f32[32,512,64]{2,1,0:T(8,128)} %bitcast.21, f32[32,64,64]{2,1,0:T(8,128)} %bitcast.22, f32[64,64]{1,0:T(8,128)} %bitcast.24, f32[64,64]{1,0:T(8,128)} %bitcast.25, f32[64,64]{1,0:T(8,128)} %bitcast.26, ...), custom_call_target="tpu_custom_call" | custom-call | tf_op jit(solution)/shard_map/pallas_call | solution.py:515
  54.7 1.9 %shard_map.113 = (f32[32,16,64]{2,1,0:T(8,128)}, f32[4,16,64]{2,1,0:T(8,128)}, f32[32,16,64]{2,1,0:T(8,128)}) custom-call(f32[16,16,128]{2,1,0:T(8,128)} %get-tuple-element.9.lw_ref, f32[2,16,128]{2,1,0:T(8,128)} %get-tuple-element.10.nw_ref, f32[16,16,128]{2,1,0:T(8,128)} %get-tuple-element.11.cp_ref), custom_call_target="tpu_custom_call" | custom-call | tf_op jit(solution)/shard_map/pallas_call | solution.py:575

commit v6 on v5

--- a/solution.py
+++ b/solution.py
@@ -105,6 +105,7 @@
     moves,
     moved,
     x_buf,
+    stage,
     onehot,
     gram_rows,
     cols,
@@ -187,11 +188,21 @@
         pl.semaphore_signal(barrier, inc=1, device_id={"clu": other(me, bit)}, device_id_type=pl.DeviceIdType.MESH)
     pl.semaphore_wait(barrier, n_rk - 1 + bits)
 
-    base_copies = [
-        to_rk(bases_ref.at[pl.ds(rk_peer(d) * group, group)], bas.at[q], bas_s, bas_r, d) for d in range(1, n_rk)
-    ]
-    for copy in base_copies:
-        copy.start()
+    part = group // 2
+
+    def base_copy(h, d):
+        return pltpu.make_async_remote_copy(
+            src_ref=bases_ref.at[pl.ds(rk_peer(d) * group + h * part, part)],
+            dst_ref=bas.at[q, pl.ds(h * part, part)],
+            send_sem=bas_s.at[h, d],
+            recv_sem=bas_r.at[h, d],
+            device_id={"rk": rk_peer(d)},
+            device_id_type=pl.DeviceIdType.MESH,
+        )
+
+    for h in range(2):
+        for d in range(1, n_rk):
+            base_copy(h, d).start()
 
     entry = lax.broadcasted_iota(jnp.int32, (1, listed), 1)
     targets = []
@@ -209,22 +220,21 @@
             onehot[first : first + size, tile * 128 : (tile + 1) * 128] = hit
 
     def prepare(j):
-        for p in range(pairs):
-            even = coup[j, pl.ds(p, listed, stride=width), :]
-            odd = coup[j, pl.ds(p + pairs, listed, stride=width), :]
-            high, low = split(jnp.concatenate([even, odd], axis=1))
-            x_buf[j, p * listed : (p + 1) * listed, :lanes] = high
-            x_buf[j, p * listed : (p + 1) * listed, lanes:] = low
-
-    early = LOADS - 1
-    for c in range(early):
+        block = coup[j].reshape(listed, 2, pairs, rank)
+        wide = jnp.concatenate([block[:, h].reshape(listed * pairs, rank) for h in range(2)], axis=1)
+        high, low = split(wide)
+        x_buf[j, :, :lanes] = high
+        x_buf[j, :, lanes:] = low
+
+    for c in range(LOADS):
         loads[c].wait()
-        pl.loop(c * blocks, (c + 1) * blocks)(prepare)
+        pl.loop(c * blocks, (c + 1) * blocks, unroll=2)(prepare)
 
     own_bases.wait()
-    for copy in base_copies:
-        copy.wait()
     for m in range(group):
+        if m % part == 0:
+            for d in range(1, n_rk):
+                base_copy(m // part, d).wait()
         whole = bas[:, m].reshape(rank, bas.shape[-1])
         gram = dot_nt(whole, whole)
         grams[m] = gram
@@ -241,10 +251,6 @@
             g1[q] = packed_rows(dot_tn(moves[...].reshape(tall), moved[...].reshape(tall)))
             for copy in g1_copies:
                 copy.start()
-        for j in range(early * blocks + n * blocks * 8 // rank, early * blocks + (n + 1) * blocks * 8 // rank):
-            if j % blocks == 0:
-                loads[j // blocks].wait()
-            prepare(j)
 
     factor_batch(rank, gram_rows, cols, upper, first_level)
     for m in range(group):
@@ -284,11 +290,12 @@
             )
             high, low = split(factor)
             prod = dot(x_buf[j], jnp.concatenate([high, high], axis=0)) + dot(x_buf[j, :, :lanes], low)
-            high, low = split(prod)
+            stage[i] = prod
             rows = pl.ds(pl.multiple_of(j * listed, listed), listed)
             for p in range(pairs):
-                p_high[rows, p * lanes : (p + 1) * lanes] = high[p * listed : (p + 1) * listed]
-                p_low[rows, p * lanes : (p + 1) * lanes] = low[p * listed : (p + 1) * listed]
+                high, low = split(stage[i, pl.ds(p, listed, stride=pairs), :])
+                p_high[rows, p * lanes : (p + 1) * lanes] = high
+                p_low[rows, p * lanes : (p + 1) * lanes] = low
 
     def level_copy(bit):
         return pltpu.make_async_remote_copy(
@@ -527,6 +534,7 @@
             pltpu.VMEM((group, rank, rank), F32),
             pltpu.VMEM((group, rank, rank), F32),
             pltpu.VMEM((leaves, listed * pairs, 4 * rank), BF16),
+            pltpu.VMEM((group, listed * pairs, 2 * rank), F32),
             pltpu.VMEM((n_clu * leaves, count), BF16),
             pltpu.VMEM((rank * BATCH, rank), F32),
             pltpu.VMEM((rank * BATCH // 128, rank, 128), F32),
@@ -544,8 +552,8 @@
             pltpu.VMEM((3, rank // 2, 2 * rank), F32),
             pltpu.VMEM((4, rank, rank), F32),
             dma((LOADS + 2,)),
-            dma((n_rk,)),
-            dma((n_rk,)),
+            dma((2, n_rk)),
+            dma((2, n_rk)),
             dma((n_rk,)),
             dma((n_rk,)),
             dma((n_rk,)),

time: 56.8 us -> 56.2 us (0.989)
  no operation moved by 1% of the time
where the time goes in v6:
time: 56.2 us; the launch traced here: 56 us
  Pallas kernels  55.4 us (99%)
  between operations  0.64 us (1%)
    pallas_call x1, Pallas kernels, shards(): pl.pallas_call(functools.partial(kernel, n_clu, n_rk, leaves, listed, wid...  53.5 us
    pallas_call x1, Pallas kernels, shards(): pl.pallas_call(unpack, out_shape=tuple((jax.ShapeDtypeStruct((2 * x.shape...  1.89 us

profile of v6, /device:TPU:0, one launch (start us, length us, event | category | flops | bytes accessed | tf_op | source)
XLA Modules:
  0.0 56.0 jit_solution(14559750526306386497)
XLA Ops:
  0.6 53.5 %shard_map.112 = (f32[16,16,128]{2,1,0:T(8,128)}, f32[2,16,128]{2,1,0:T(8,128)}, f32[16,16,128]{2,1,0:T(8,128)}) custom-call(f32[32,16,256]{2,1,0:T(8,128)} %bitcast.23, f32[32,512,64]{2,1,0:T(8,128)} %bitcast.21, f32[32,64,64]{2,1,0:T(8,128)} %bitcast.22, f32[64,64]{1,0:T(8,128)} %bitcast.24, f32[64,64]{1,0:T(8,128)} %bitcast.25, f32[64,64]{1,0:T(8,128)} %bitcast.26, ...), custom_call_target="tpu_custom_call" | custom-call | tf_op jit(solution)/shard_map/pallas_call | solution.py:522
  54.1 1.9 %shard_map.113 = (f32[32,16,64]{2,1,0:T(8,128)}, f32[4,16,64]{2,1,0:T(8,128)}, f32[32,16,64]{2,1,0:T(8,128)}) custom-call(f32[16,16,128]{2,1,0:T(8,128)} %get-tuple-element.9.lw_ref, f32[2,16,128]{2,1,0:T(8,128)} %get-tuple-element.10.nw_ref, f32[16,16,128]{2,1,0:T(8,128)} %get-tuple-element.11.cp_ref), custom_call_target="tpu_custom_call" | custom-call | tf_op jit(solution)/shard_map/pallas_call | solution.py:583
